TPU v7x, 256 devices: a whole 4x4x8 slice. The times are simulated.
256 devices in a mesh: dp: 32 (over z, y), ctx: 4 (over x), side: 2 (over core).
Axes of the slice: x: 4, y: 4, z: 8, core: 2. Of those that a mesh axis runs over, the one named last changes fastest.
Arguments:
- queries: bfloat16 [64, 8192], P('dp'), may hold values from -70 to 70
- new_key: bfloat16 [64, 1024], P('dp'), may hold values from -40 to 40
- new_value: bfloat16 [64, 1024], P('dp'), may hold values from -6 to 6
- key_pool: bfloat16 [6144, 64, 1024], P(('dp', 'ctx', 'side')), may hold values from -40 to 40
- value_pool: bfloat16 [6144, 64, 1024], P(('dp', 'ctx', 'side')), may hold values from -6 to 6
- page_table: int32 [32, 8, 24], P('dp', ('ctx', 'side')), may hold values from 0 to 23, each once within a row
- lengths: int32 [64], P('dp'), may hold values from 1 to 6144, as said below
- residual: bfloat16 [64, 8192], P(None, 'dp'), may hold values from -40 to 40
- out_weight: bfloat16 [8192, 8192], P(('ctx', 'side'), 'dp'), may hold values from -0.5 to 0.5
- norm_gain: float32 [8192], P('dp'), may hold values from 0.1 to 1.9
- gate_weight: bfloat16 [8192, 28672], P('dp', ('ctx', 'side')), may hold values from -0.0625 to 0.0625
- up_weight: bfloat16 [8192, 28672], P('dp', ('ctx', 'side')), may hold values from -0.0625 to 0.0625
- down_weight: bfloat16 [28672, 8192], P(('ctx', 'side'), 'dp'), may hold values from -0.03125 to 0.03125
Outputs:
- layer_out: bfloat16 [64, 8192], P(('ctx', 'side'), 'dp')
Inputs may be any that keep to these rules, and one draw needn't show every extreme that they name: `lengths`: cached tokens of each row; the new token comes after them.
All inputs are finite; a program needn't handle non-finite values.
Results may differ from a plain program's by a relative error of at most 0.018.
Values may be sent and summed in bfloat16 or wider, within the bound.
No kernel may reach another device: no remote copies, remote signals or barrier semaphores. Data moves between devices by JAX's collectives and lax.ppermute only.
A program may use at most 64 MiB of HBM per device.

v0:
```python
import math

import jax
import jax.numpy as jnp
from jax import lax
from jax.sharding import PartitionSpec as P

D = 8192
KVH = 8
HD = 128
PAGE = 64
PMAX = 12
G = 8


norm_eps = 1e-05


def combined_all(part, axis, combine):
    gathered = jax.tree.map(lambda a: lax.all_gather(a, axis), part)

    def take(source):
        return jax.tree.map(lambda a: lax.dynamic_index_in_dim(a, source, 0, False), gathered)

    return lax.fori_loop(
        1, lax.axis_size(axis), lambda source, state: combine(state, take(source)), take(0)
    )


def merge_parts(first, second):
    peak_first, total_first, weighted_first = first
    peak_second, total_second, weighted_second = second
    peak_both = jnp.maximum(peak_first, peak_second)
    factor_first = jnp.exp(peak_first - peak_both)
    factor_second = jnp.exp(peak_second - peak_both)
    weight_total = total_first * factor_first + total_second * factor_second
    weighted = weighted_first * factor_first[..., None] + weighted_second * factor_second[..., None]
    return (peak_both, weight_total, weighted)


def body(
    queries,
    new_key,
    new_value,
    key_pool,
    value_pool,
    page_table,
    lengths,
    residual,
    out_weight,
    norm_gain,
    gate_weight,
    up_weight,
    down_weight,
):
    row_count = queries.shape[0]
    shards = lax.axis_size(("ctx", "side"))
    shard_index = lax.axis_index(("ctx", "side"))
    score_scale = 1.0 / math.sqrt(HD)
    slot_ids = page_table[0, 0, : row_count * PMAX].reshape(row_count, PMAX)
    gathered_keys = key_pool[slot_ids].reshape(row_count, PMAX * PAGE, KVH, HD)
    gathered_values = value_pool[slot_ids].reshape(row_count, PMAX * PAGE, KVH, HD)
    query_heads = queries.reshape(row_count, KVH, G, HD)
    scores = (
        jnp.einsum(
            "rhgd,rthd->rhgt", query_heads, gathered_keys, preferred_element_type=jnp.float32
        )
        * score_scale
    )
    tokens_here = jnp.arange(PMAX * PAGE, dtype=jnp.int32)
    positions = (tokens_here // PAGE * shards + shard_index) * PAGE + tokens_here % PAGE
    live_mask = positions[None, :] < lengths[:, None]
    scores = jnp.where(live_mask[:, None, None, :], scores, jnp.float32(-1e30))
    peak_score = jnp.max(scores, axis=-1)
    weights = (
        jnp.exp(scores - peak_score[..., None]) * live_mask.astype(jnp.float32)[:, None, None, :]
    )
    weight_total = jnp.sum(weights, axis=-1)
    rounded_weights = weights.astype(jnp.bfloat16)
    weighted = jnp.einsum(
        "rhgt,rthd->rhgd", rounded_weights, gathered_values, preferred_element_type=jnp.float32
    )
    fresh_score = (
        jnp.einsum(
            "rhgd,rhd->rhg",
            query_heads,
            new_key.reshape(row_count, KVH, HD),
            preferred_element_type=jnp.float32,
        )
        * score_scale
    )
    fresh_score = lax.dynamic_slice_in_dim(fresh_score, shard_index, 1, 1)
    fresh_value = lax.dynamic_slice_in_dim(
        new_value.reshape(row_count, KVH, HD), shard_index, 1, 1
    ).astype(jnp.float32)
    merged = combined_all((peak_score, weight_total, weighted), ("ctx", "side"), merge_parts)
    peak_own = lax.dynamic_slice_in_dim(merged[0], shard_index, 1, 1)
    total_own = lax.dynamic_slice_in_dim(merged[1], shard_index, 1, 1)
    weighted_own = lax.dynamic_slice_in_dim(merged[2], shard_index, 1, 1)
    peak_final = jnp.maximum(peak_own, fresh_score)
    factor_old = jnp.exp(peak_own - peak_final)
    fresh_weight = jnp.exp(fresh_score - peak_final)
    total_final = total_own * factor_old + fresh_weight
    weighted_final = (
        weighted_own * factor_old[..., None] + fresh_weight[..., None] * fresh_value[:, :, None, :]
    )
    attended = (
        (weighted_final / total_final[..., None]).reshape(row_count, G * HD).astype(jnp.bfloat16)
    )
    partial_proj = jnp.dot(
        lax.all_gather(attended, "dp", axis=0, tiled=True),
        out_weight,
        preferred_element_type=jnp.float32,
    )
    projected = lax.psum(partial_proj, ("ctx", "side"))
    middle_f = (residual.astype(jnp.float32) + projected).astype(jnp.bfloat16).astype(jnp.float32)
    scaled = (middle_f * norm_gain[None, :]).astype(jnp.bfloat16)
    gate_part = jnp.dot(scaled, gate_weight, preferred_element_type=jnp.float32)
    up_part = jnp.dot(scaled, up_weight, preferred_element_type=jnp.float32)
    squares = jnp.sum(middle_f * middle_f, axis=1)
    gate_sum, up_sum, square_sum = lax.psum((gate_part, up_part, squares), "dp")
    inverse = 1.0 / jnp.sqrt(square_sum / D + norm_eps)
    hidden = (jax.nn.silu(gate_sum * inverse[:, None]) * (up_sum * inverse[:, None])).astype(
        jnp.bfloat16
    )
    share_rows = hidden.shape[0] // shards
    down_part = lax.psum_scatter(
        jnp.dot(hidden, down_weight, preferred_element_type=jnp.float32),
        ("ctx", "side"),
        scatter_dimension=0,
        tiled=True,
    )
    middle_own = lax.dynamic_slice_in_dim(middle_f, shard_index * share_rows, share_rows, 0)
    return (middle_own + down_part).astype(jnp.bfloat16)


def solution(mesh):
    placed = (
        P("dp", None),
        P("dp", None),
        P("dp", None),
        P(("dp", "ctx", "side"), None, None),
        P(("dp", "ctx", "side"), None, None),
        P("dp", ("ctx", "side"), None),
        P("dp"),
        P(None, "dp"),
        P(("ctx", "side"), "dp"),
        P("dp"),
        P("dp", ("ctx", "side")),
        P("dp", ("ctx", "side")),
        P(("ctx", "side"), "dp"),
    )
    return jax.shard_map(
        body, mesh=mesh, in_specs=placed, out_specs=P(("ctx", "side"), "dp"), check_vma=False
    )
```

profile of v0, /device:TPU:1, one launch (start us, length us, event | category | flops | bytes accessed | tf_op | source)
XLA Modules:
  0.0 378.8 jit_solution(11449091288505937955)
XLA Ops:
  7.1 1.6 reduce.3
  8.9 2.5 gather_fusion
  11.4 4.4 %copy.22 = bf16[192,8,8,128]{3,2,1,0:T(8,128)(2,1)} copy(bf16[192,8,8,128]{3,1,2,0:T(8,128)(2,1)} %bitcast.64) | data formatting | bytes 6291456
  15.8 4.4 %gather_fusion.1 = bf16[24,64,1024]{2,1,0:T(8,128)(2,1)} fusion(bf16[24,64,1024]{2,1,0:T(8,128)(2,1)} %param.19, s32[1024]{0:T(1024)S(1)} %pad_clamp_fusion), kind=kCustom, calls=%fused_computation.1 | custom fusion | bytes 6291552 | tf_op jit(solution)/shard_map/gather | solution.py:62
  20.2 2.9 copy.24
  23.2 1.0 fusion.54
  24.2 15.8 %all-gather = f32[16,8,8]{2,1,0:T(8,128)S(1)} all-gather(f32[2,8,8]{2,1,0:T(8,128)S(1)} %get-tuple-element.213), channel_id=2, replica_groups=mesh['dp'=32,'ctx'=4,'side'=2] {'ctx','side'}, dimensions={0}, use_global_device_ids=true | all-gather | bytes 4608 | tf_op jit(solution)/shard_map/all_gather | solution.py:20
  40.9 13.1 %all-gather.2 = f32[16,8,8,128]{3,2,1,0:T(8,128)S(1)} all-gather(f32[2,8,8,128]{3,2,1,0:T(8,128)S(1)} %fusion.3), channel_id=4, replica_groups=mesh['dp'=32,'ctx'=4,'side'=2] {'ctx','side'}, dimensions={0}, use_global_device_ids=true | all-gather | bytes 589824 | tf_op jit(solution)/shard_map/all_gather | solution.py:20
  54.1 12.7 %all-gather.1 = f32[16,8,8]{2,1,0:T(8,128)S(1)} all-gather(f32[2,8,8]{2,1,0:T(8,128)S(1)} %fusion.18), channel_id=3, replica_groups=mesh['dp'=32,'ctx'=4,'side'=2] {'ctx','side'}, dimensions={0}, use_global_device_ids=true | all-gather | bytes 4608 | tf_op jit(solution)/shard_map/all_gather | solution.py:20
  66.8 7.0 %while.19 = (s32[]{:T(128)}, f32[2,8,8]{2,1,0:T(8,128)S(1)}, f32[2,8,8]{2,1,0:T(8,128)S(1)}, f32[2,8,8,128]{3,2,1,0:T(8,128)S(1)}, f32[8,2,8,8]{3,2,1,0:T(8,128)...) while((s32[]{:T(128)}, f32[2,8,8]{2,1,0:T(8,128)S(1)}, ...), condition=%wide.region_3.4_spmd, body=%wide.region_2.3_spmd.sunk | while | flops 49925 | bytes 201879 | solution.py:25
  66.9 1.0 fusion.65
  67.9 1.0 fusion.65
  69.9 1.0 fusion.65
  74.8 35.2 %all-gather.3 = bf16[32,2,1024]{2,1,0:T(2,128)(2,1)S(1)} all-gather(bf16[1,2,1024]{2,1,0:T(2,128)(2,1)S(1)} %reshape.170), channel_id=1, replica_groups=mesh['dp'=32,'ctx'=4,'side'=2] {'dp'}, dimensions={0}, use_global_device_ids=true | all-gather | bytes 135168 | tf_op jit(solution)/shard_map/all_gather | solution.py:111
  110.1 1.9 fusion.55
  112.0 68.3 %all-reduce.4.cloned.1.call-done = f32[64,256]{1,0:T(8,128)} async-done(((f32[64,256]{1,0:T(8,128)}), f32[64,256]{1,0:T(8,128)}) %all-reduce.4.cloned.1.call-update) | async-done | bytes 65552 | tf_op jit(solution)/shard_map/psum | solution.py:115
  180.3 1.1 multiply_reduce_fusion
  181.4 2.9 fusion.28
  184.3 1.4 fusion.29
  185.8 61.3 %psum.30 = f32[64]{0:T(128)S(1)} all-reduce(f32[64]{0:T(128)S(1)} %get-tuple-element.206), channel_id=1, replica_groups=mesh['dp'=32,'ctx'=4,'side'=2] {'dp'}, use_global_device_ids=true, to_apply=%region_7.8 | all-reduce | flops 64 | bytes 512 | tf_op jit(solution)/shard_map/psum | solution.py:121
  247.0 89.0 %all-reduce.6.cloned.1.call-done = (f32[64,3584]{1,0:T(8,128)}, f32[64,3584]{1,0:T(8,128)}) async-done(((f32[64,3584]{1,0:T(8,128)}, f32[64,3584]{1,0:T(8,128)}), (f32[64,3584]{1,0:T(8,128)}, f32[64,3584]{1,0:T(8,128)})) %all-reduce.6.cloned.1.call-update) | async-done | bytes 1835024 | tf_op jit(solution)/shard_map/psum | solution.py:121
  336.0 3.2 fusion.16
  339.2 31.7 %reduce-scatter.2.cloned.1.call-done = f32[8,256]{1,0:T(8,128)} async-done(((f32[64,256]{1,0:T(8,128)}), f32[8,256]{1,0:T(8,128)}) %reduce-scatter.2.cloned.1.call-update) | async-done | bytes 8208 | tf_op jit(solution)/shard_map/reduce_scatter | solution.py:127
  371.0 1.3 add_convert_fusion.1
  (55 shorter events, 6.9 us)
Async XLA Ops:
  6.5 2.4 copy-start
  6.5 173.8 %all-reduce.4.cloned.1.call-start = ((), (), s32[]{:S(2)}) async-start(), calls=%async_computation.1 | async-start | bytes 131072 | tf_op jit(solution)/shard_map/psum | solution.py:115
  20.2 2.9 copy-start.7
  20.2 3.0 copy-start.1
  20.2 3.0 copy-start.8
  40.2 33.6 %copy-start.6 = (bf16[2,1024]{1,0:T(2,128)(2,1)S(1)}, bf16[2,1024]{1,0:T(2,128)(2,1)}, u32[]{:S(2)}) copy-start(bf16[2,1024]{1,0:T(2,128)(2,1)} %param.16) | copy-start | bytes 12292
  40.2 140.1 %copy-start.4 = (bf16[64,256]{1,0:T(8,128)(2,1)S(1)}, bf16[64,256]{1,0:T(8,128)(2,1)}, u32[]{:S(2)}) copy-start(bf16[64,256]{1,0:T(8,128)(2,1)} %param.22) | copy-start | bytes 98308
  40.2 141.2 %copy-start.5 = (f32[256]{0:T(256)S(1)}, f32[256]{0:T(256)}, u32[]{:S(2)}) copy-start(f32[256]{0:T(256)} %param.24) | copy-start | bytes 3076
  54.1 12.7 %copy-start.3 = (f32[16,8,8,128]{3,2,1,0:T(8,128)}, f32[16,8,8,128]{3,2,1,0:T(8,128)S(1)}, u32[]{:S(2)}) copy-start(f32[16,8,8,128]{3,2,1,0:T(8,128)S(1)} %all-gather.2) | copy-start | bytes 1572868
  112.0 224.0 %all-reduce.6.cloned.1.call-start = ((), (), s32[]{:S(2)}) async-start(), calls=%async_computation.3 | async-start | bytes 3670016 | tf_op jit(solution)/shard_map/psum | solution.py:121
  180.3 4.0 %copy-start.2 = (bf16[256,3584]{1,0:T(8,128)(2,1)S(1)}, bf16[256,3584]{1,0:T(8,128)(2,1)}, u32[]{:S(2)}) copy-start(bf16[256,3584]{1,0:T(8,128)(2,1)} %param.25) | copy-start | bytes 5505028
  185.7 185.3 %reduce-scatter.2.cloned.1.call-start = ((), (), s32[]{:S(2)}) async-start(), calls=%async_computation.2 | async-start | bytes 73728 | tf_op jit(solution)/shard_map/reduce_scatter | solution.py:127
Sparse Core Ops, SparseCore 0:
  112.1 68.1 all-reduce.3
  185.8 150.1 all-reduce.5
  339.4 31.5 reduce-scatter.1
where the time goes:
time: 381 us; the launch traced here: 379 us
  waiting for transfers between devices  189 us (50%)
  blocking collectives  138 us (36%)
  local copies, waits for them, and re-layouts  15 us (4%)
  between operations  13.2 us (3%)
  other arithmetic  11.9 us (3%)
  matrix products  11.1 us (3%)
    psum x1, waiting for transfers between devices, body(): gate_sum, up_sum, square_sum = lax.psum((gate_part, up_part, squares), 'dp')  89 us
    psum x1, waiting for transfers between devices, body(): projected = lax.psum(partial_proj, ('ctx', 'side'))  68.3 us
    psum x1, blocking collectives, body(): gate_sum, up_sum, square_sum = lax.psum((gate_part, up_part, squares), 'dp')  61.3 us
    all_gather x3, blocking collectives, combined_all(): gathered = jax.tree.map(lambda a: lax.all_gather(a, axis), part)  41.7 us
    all_gather x1, blocking collectives, body(): lax.all_gather(attended, 'dp', axis=0, tiled=True)  35.2 us
    reduce_scatter x1, waiting for transfers between devices, body(): lax.psum_scatter(jnp.dot(hidden, down_weight, preferred_element_type=jnp....  31.7 us
    unnamed x23, local copies, waits for them, and re-layouts  7.91 us
  transfers between devices with their start and end apart: 3, of which 3 were waited for; matrix products, arithmetic and copies ran while one was open for 0% of the time, Pallas kernels for 0%

commit v1 on v0

v1 whole, which is shorter than its diff:
```python
import functools
import math

import jax
import jax.numpy as jnp
from jax import lax
from jax.experimental import pallas as pl
from jax.experimental.pallas import tpu as pltpu
from jax.sharding import PartitionSpec as P

D = 8192
KVH = 8
HD = 128
PAGE = 64
PMAX = 12
G = 8
ROWS_DEV = 2
SLOTS = ROWS_DEV * PMAX
TOKENS = SLOTS * PAGE
QROWS = ROWS_DEV * KVH * G
CHUNKS = 4
CHUNK = TOKENS // CHUNKS
NEG = -1e30
SHARD_AXES = ("ctx", "side")

norm_eps = 1e-05
f32 = jnp.float32
bf16 = jnp.bfloat16


def attend_kernel(
    table, lengths, q_ref, nk_ref, nv_ref, key_hbm, value_hbm, out_ref,
    keys, values, q_wide, scores, owner, key_sem, value_sem,
):
    shard = lax.axis_index(SHARD_AXES)

    def copy(src, dst, sem, c):
        rows = pl.ds(c * CHUNK, CHUNK)
        return pltpu.make_async_copy(src.at[rows], dst.at[rows], sem.at[c])

    for c in range(CHUNKS):
        copy(key_hbm, keys, key_sem, c).start()
    for c in range(CHUNKS):
        copy(value_hbm, values, value_sem, c).start()

    for k in range(SLOTS):
        owner[table[0, 0, k]] = k

    def limit_of(slot, row):
        k = owner[slot]
        own = lax.div(k, PMAX)
        page = lax.rem(k, PMAX)
        start = (page * 8 + shard) * PAGE
        count = lengths[row] - start
        return jnp.where(own == row, count, 0)

    q = q_ref[...]
    head_of_row = lax.rem(lax.div(lax.broadcasted_iota(jnp.int32, (QROWS, HD), 0), G), KVH)
    for h in range(KVH):
        q_wide[:, h * HD : (h + 1) * HD] = jnp.where(head_of_row == h, q, jnp.zeros_like(q))

    scale = 1.0 / math.sqrt(HD)

    def per_group(ref):
        parts = []
        for r in range(ROWS_DEV):
            for h in range(KVH):
                one = ref[r : r + 1, h * HD : (h + 1) * HD].astype(f32)
                parts.append(jnp.broadcast_to(one, (G, HD)))
        return jnp.concatenate(parts, axis=0)

    fresh = jnp.sum(q.astype(f32) * per_group(nk_ref), axis=1, keepdims=True) * scale
    fresh = jnp.where(shard == 0, fresh, NEG)
    new_values = per_group(nv_ref)

    lane = lax.broadcasted_iota(jnp.int32, (QROWS // ROWS_DEV, HD), 1)
    within = lax.rem(lane, PAGE)
    first_half = lane < PAGE
    peak = fresh
    for c in range(CHUNKS):
        copy(key_hbm, keys, key_sem, c).wait()
        part = lax.dot_general(
            q_wide[...], keys[c * CHUNK : (c + 1) * CHUNK, :],
            (((1,), (1,)), ((), ())), preferred_element_type=f32,
        ) * scale
        for t in range(CHUNK // HD):
            slot = (c * CHUNK + t * HD) // PAGE
            tiles = []
            for r in range(ROWS_DEV):
                live = within < jnp.where(first_half, limit_of(slot, r), limit_of(slot + 1, r))
                tile = part[r * KVH * G : (r + 1) * KVH * G, t * HD : (t + 1) * HD]
                tiles.append(jnp.where(live, tile, NEG))
            tile = jnp.concatenate(tiles, axis=0)
            scores[:, c * CHUNK + t * HD : c * CHUNK + (t + 1) * HD] = tile
            peak = jnp.maximum(peak, jnp.max(tile, axis=1, keepdims=True))

    total = jnp.zeros((QROWS, HD), f32)
    mixed = jnp.zeros((QROWS, KVH * HD), f32)
    for c in range(CHUNKS):
        part = scores[:, c * CHUNK : (c + 1) * CHUNK]
        weight = jnp.where(part > 0.5 * NEG, jnp.exp(part - peak), 0.0)
        for t in range(CHUNK // HD):
            total = total + weight[:, t * HD : (t + 1) * HD]
        copy(value_hbm, values, value_sem, c).wait()
        mixed = mixed + jnp.dot(
            weight.astype(bf16), values[c * CHUNK : (c + 1) * CHUNK, :], preferred_element_type=f32
        )
    fresh_weight = jnp.where(shard == 0, jnp.exp(fresh - peak), 0.0)
    total = jnp.sum(total, axis=1, keepdims=True) + fresh_weight
    added = fresh_weight * new_values
    stat_lane = lax.broadcasted_iota(jnp.int32, (QROWS, HD), 1)
    stats = jnp.where(stat_lane == 0, peak, total)
    for h in range(KVH):
        for r in range(ROWS_DEV):
            at = (r * KVH + h) * G
            own = mixed[at : at + G, h * HD : (h + 1) * HD] + added[at : at + G, :]
            out_ref[h, r * G : (r + 1) * G, 0:HD] = own
            out_ref[h, r * G : (r + 1) * G, HD : 2 * HD] = stats[at : at + G, :]


def attend(table, lengths, q, new_key, new_value, keys, values):
    smem = pl.BlockSpec(memory_space=pltpu.SMEM)
    vmem = pl.BlockSpec(memory_space=pltpu.VMEM)
    hbm = pl.BlockSpec(memory_space=pl.ANY)
    return pl.pallas_call(
        attend_kernel,
        out_shape=jax.ShapeDtypeStruct((KVH, ROWS_DEV * G, 2 * HD), f32),
        in_specs=[smem, smem, vmem, vmem, vmem, hbm, hbm],
        out_specs=vmem,
        scratch_shapes=[
            pltpu.VMEM((TOKENS, KVH * HD), bf16),
            pltpu.VMEM((TOKENS, KVH * HD), bf16),
            pltpu.VMEM((QROWS, KVH * HD), bf16),
            pltpu.VMEM((QROWS, TOKENS), f32),
            pltpu.SMEM((SLOTS,), jnp.int32),
            pltpu.SemaphoreType.DMA((CHUNKS,)),
            pltpu.SemaphoreType.DMA((CHUNKS,)),
        ],
        compiler_params=pltpu.CompilerParams(vmem_limit_bytes=24 * 1024 * 1024),
        name="attend",
    )(table, lengths, q, new_key, new_value, keys, values)


def merge_kernel(parts_ref, out_ref, wide):
    shards = parts_ref.shape[0]
    peak = parts_ref[0, :, HD : HD + 1]
    for s in range(1, shards):
        peak = jnp.maximum(peak, parts_ref[s, :, HD : HD + 1])
    total = jnp.zeros_like(peak)
    mixed = jnp.zeros((ROWS_DEV * G, HD), f32)
    for s in range(shards):
        factor = jnp.exp(parts_ref[s, :, HD : HD + 1] - peak)
        total = total + factor * parts_ref[s, :, HD + 1 : HD + 2]
        mixed = mixed + factor * parts_ref[s, :, 0:HD]
    attended = mixed / total
    for r in range(ROWS_DEV):
        for g in range(G):
            wide[r : r + 1, g * HD : (g + 1) * HD] = attended[r * G + g : r * G + g + 1, :]
    out_ref[...] = wide[0:ROWS_DEV, :].astype(bf16)


def merge(parts):
    vmem = pl.BlockSpec(memory_space=pltpu.VMEM)
    return pl.pallas_call(
        merge_kernel,
        out_shape=jax.ShapeDtypeStruct((ROWS_DEV, G * HD), bf16),
        in_specs=[vmem],
        out_specs=vmem,
        scratch_shapes=[pltpu.VMEM((8, G * HD), f32)],
        name="merge",
    )(parts)


def gather(x, axes):
    copies = jnp.broadcast_to(x[None], (lax.axis_size(axes),) + x.shape)
    return lax.all_to_all(copies, axes, 0, 0)


def body(
    queries,
    new_key,
    new_value,
    key_pool,
    value_pool,
    page_table,
    lengths,
    residual,
    out_weight,
    norm_gain,
    gate_weight,
    up_weight,
    down_weight,
):
    shards = lax.axis_size(SHARD_AXES)
    groups = lax.axis_size("dp")
    shard_index = lax.axis_index(SHARD_AXES)
    rows = residual.shape[0]
    hidden_here = gate_weight.shape[1]

    parts = attend(
        page_table,
        lengths,
        queries.reshape(QROWS, HD),
        new_key,
        new_value,
        key_pool.reshape(TOKENS, KVH * HD),
        value_pool.reshape(TOKENS, KVH * HD),
    )
    attended = merge(lax.all_to_all(parts, SHARD_AXES, 0, 0))
    attended = gather(attended, "dp").reshape(rows, G * HD)
    partial_proj = jnp.dot(attended, out_weight, preferred_element_type=f32).astype(bf16)
    projected = jnp.sum(gather(partial_proj, SHARD_AXES).astype(f32), axis=0)
    middle = (residual.astype(f32) + projected).astype(bf16)
    middle_f = middle.astype(f32)
    scaled = (middle_f * norm_gain[None, :]).astype(bf16)
    squares = jnp.sum(middle_f * middle_f, axis=1, keepdims=True)
    squares_high = squares.astype(bf16)
    squares_low = (squares - squares_high.astype(f32)).astype(bf16)
    gate_part = jnp.dot(scaled, gate_weight, preferred_element_type=f32).astype(bf16)
    up_part = jnp.dot(scaled, up_weight, preferred_element_type=f32).astype(bf16)
    pad = jnp.zeros((rows, HD - 2), bf16)
    sent = jnp.concatenate([gate_part, up_part, squares_high, squares_low, pad], axis=1)
    came = lax.all_to_all(
        sent.reshape(groups, ROWS_DEV, sent.shape[1]), "dp", 0, 0
    )
    sums = jnp.sum(came.astype(f32), axis=0)
    square_sum = sums[:, 2 * hidden_here] + sums[:, 2 * hidden_here + 1]
    inverse = (1.0 / jnp.sqrt(square_sum / D + norm_eps))[:, None]
    gate = sums[:, :hidden_here] * inverse
    up = sums[:, hidden_here : 2 * hidden_here] * inverse
    hidden = (jax.nn.silu(gate) * up).astype(bf16)
    hidden = gather(hidden, "dp").reshape(rows, hidden_here)
    down = jnp.dot(hidden, down_weight, preferred_element_type=f32)
    share_rows = rows // shards
    down = lax.all_to_all(down.reshape(shards, share_rows, down.shape[1]), SHARD_AXES, 0, 0)
    middle_own = lax.dynamic_slice_in_dim(middle_f, shard_index * share_rows, share_rows, 0)
    return (middle_own + jnp.sum(down, axis=0)).astype(bf16)


def solution(mesh):
    placed = (
        P("dp", None),
        P("dp", None),
        P("dp", None),
        P(("dp", "ctx", "side"), None, None),
        P(("dp", "ctx", "side"), None, None),
        P("dp", ("ctx", "side"), None),
        P("dp"),
        P(None, "dp"),
        P(("ctx", "side"), "dp"),
        P("dp"),
        P("dp", ("ctx", "side")),
        P("dp", ("ctx", "side")),
        P(("ctx", "side"), "dp"),
    )
    return jax.shard_map(
        body, mesh=mesh, in_specs=placed, out_specs=P(("ctx", "side"), "dp"), check_vma=False
    )
```

time: 381 us -> 130 us (0.34)
  waiting for transfers between devices: 189 us -> 4.87 us
  blocking collectives: 138 us -> 89 us
  between operations: 13.2 us -> 0.17 us
  other arithmetic: 11.9 us -> 1.84 us
  starting transfers between devices: 0.09 us -> 7.44 us
  Pallas kernels: 0 us -> 6.05 us
  matrix products: 11.1 us -> 5.14 us
    psum x2 -> x0, waiting for transfers between devices: 157 us -> none  [the longest x1 89 us: body(): gate_sum, up_sum, square_sum = lax.psum((gate_part, up_part, squares), 'dp')]
    all_to_all x0 -> x5, blocking collectives: none -> 89 us  [the longest x3 50.7 us: gather(): return lax.all_to_all(copies, axes, 0, 0)]
    all_gather x4 -> x0, blocking collectives: 76.9 us -> none  [the longest x3 41.7 us: combined_all(): gathered = jax.tree.map(lambda a: lax.all_gather(a, axis), part)]
    psum x1 -> x0, blocking collectives: 61.3 us -> none  [body(): gate_sum, up_sum, square_sum = lax.psum((gate_part, up_part, squares), 'dp')]
    reduce_scatter x1 -> x0, waiting for transfers between devices: 31.7 us -> none  [body(): lax.psum_scatter(jnp.dot(hidden, down_weight, preferred_element_type=jnp....]
    all_to_all x0 -> x1, starting transfers between devices: none -> 7.44 us  [body(): lax.all_to_all(down.reshape(shards, share_rows, down.shape[1]), SHARD_AXE...]
    gather x2 -> x0, local copies, waits for them, and re-layouts: 6.95 us -> none  [the longest x1 4.42 us: body(): value_pool[slot_ids].reshape(row_count, PMAX * PAGE, KVH, HD)]
    add x16 -> x0, other arithmetic: 6.84 us -> none  [the longest x7 6.69 us: merge_parts(): weighted_first * factor_first[..., None]]
  transfers between devices with their start and end apart: 3 -> 1, of which waited for: 3 -> 1; matrix products, arithmetic and copies ran while one was open for 0% -> 0% of each run, Pallas kernels for 0% -> 0%
where the time goes in v1:
time: 130 us; the launch traced here: 129 us
  blocking collectives  89 us (68%)
  local copies, waits for them, and re-layouts  14.7 us (11%)
  starting transfers between devices  7.44 us (6%)
  Pallas kernels  6.05 us (5%)
  matrix products  5.14 us (4%)
  waiting for transfers between devices  4.87 us (4%)
  other arithmetic  1.84 us (1%)
    all_to_all x3, blocking collectives, gather(): return lax.all_to_all(copies, axes, 0, 0)  50.7 us
    all_to_all x1, blocking collectives, body(): lax.all_to_all(sent.reshape(groups, ROWS_DEV, sent.shape[1]), 'dp', 0, 0)  26.5 us
    all_to_all x1, blocking collectives, body(): attended = merge(lax.all_to_all(parts, SHARD_AXES, 0, 0))  11.7 us
    all_to_all x1, starting transfers between devices, body(): lax.all_to_all(down.reshape(shards, share_rows, down.shape[1]), SHARD_AXE...  7.44 us
    unnamed x20, local copies, waits for them, and re-layouts  6.47 us
    concatenate x3, local copies, waits for them, and re-layouts, body(): jnp.concatenate([gate_part, up_part, squares_high, squares_low, pad], axi...  5.67 us
    all_to_all x1, waiting for transfers between devices, body(): lax.all_to_all(down.reshape(shards, share_rows, down.shape[1]), SHARD_AXE...  4.87 us
    pallas_call x1, Pallas kernels, attend(): pl.pallas_call(attend_kernel, out_shape=jax.ShapeDtypeStruct((KVH, ROWS_D...  4.37 us
  transfers between devices with their start and end apart: 1, of which 1 were waited for; matrix products, arithmetic and copies ran while one was open for 0% of the time, Pallas kernels for 0%

profile of v1, /device:TPU:1, one launch (start us, length us, event | category | flops | bytes accessed | tf_op | source)
XLA Modules:
  0.0 129.2 jit_solution(12686747935774278290)
XLA Ops:
  0.0 0.9 reshape.61.q_ref
  0.9 1.9 %copy-done.1 = bf16[24,64,1024]{2,1,0:T(8,128)(2,1)S(1)} copy-done((bf16[24,64,1024]{2,1,0:T(8,128)(2,1)S(1)}, bf16[24,64,1024]{2,1,0:T(8,128)(2,1)}, u32[]{:S(2)}) %copy-start.1) | copy-done | bytes 3145752
  2.8 1.9 %copy-done.2 = bf16[24,64,1024]{2,1,0:T(8,128)(2,1)S(1)} copy-done((bf16[24,64,1024]{2,1,0:T(8,128)(2,1)S(1)}, bf16[24,64,1024]{2,1,0:T(8,128)(2,1)}, u32[]{:S(2)}) %copy-start.2) | copy-done | bytes 3145752
  4.7 0.7 copy-done.3
  5.4 0.7 copy-done.4
  6.1 0.7 copy-done.5
  6.7 0.7 copy-done.6
  7.4 4.4 %attend.1 = f32[8,16,256]{2,1,0:T(8,128)S(1)} custom-call(s32[1,1,24]{2,1,0:T(1,128)S(1)} %copy-done.5, s32[2]{0:T(128)S(1)} %copy-done.6, bf16[128,128]{1,0:T(8,128)(2,1)S(1)} %reshape.61.q_ref, bf16[2,1024]{1,0:T(2,128)(2,1)S(1)} %copy-done.3, bf16[2,1024]{1,0:T(2,128)(2,1)S(1)} %copy-done.4, bf16[1536,1024]{1,0:T(8,128)(2,1)S(1)} %bitcast.10, ...), custom_call_target="tpu_custom_call" | custom-call | tf_op jit(solution)/shard_map/attend/pallas_call | solution.py:125
  11.8 11.7 %all_to_all.30.parts_ref = f32[8,16,256]{2,1,0:T(8,128)} all-to-all(f32[8,16,256]{2,1,0:T(8,128)S(1)} %attend.1), channel_id=1, replica_groups=mesh['dp'=32,'ctx'=4,'side'=2] {'ctx','side'}, dimensions={0} | all-to-all | bytes 262144 | tf_op jit(solution)/shard_map/all_to_all | solution.py:209
  23.5 1.7 %merge.1 = bf16[2,1024]{1,0:T(2,128)(2,1)} custom-call(f32[8,16,256]{2,1,0:T(8,128)} %all_to_all.30.parts_ref), custom_call_target="tpu_custom_call" | custom-call | tf_op jit(solution)/shard_map/merge/pallas_call | solution.py:164
  25.2 0.8 broadcast_in_dim.8
  25.9 19.8 %all_to_all.31 = bf16[32,2,1024]{2,1,0:T(2,128)(2,1)S(1)} all-to-all(bf16[32,2,1024]{2,1,0:T(2,128)(2,1)S(1)} %broadcast_in_dim.8), channel_id=1, replica_groups=mesh['dp'=32,'ctx'=4,'side'=2] {'dp'}, dimensions={0} | all-to-all | bytes 262144 | tf_op jit(solution)/shard_map/all_to_all | solution.py:176
  46.0 11.2 %all_to_all.32 = bf16[8,64,256]{2,1,0:T(8,128)(2,1)S(1)} all-to-all(bf16[8,64,256]{2,1,0:T(8,128)(2,1)S(1)} %broadcast_in_dim.9), channel_id=1, replica_groups=mesh['dp'=32,'ctx'=4,'side'=2] {'ctx','side'}, dimensions={0} | all-to-all | bytes 524288 | tf_op jit(solution)/shard_map/all_to_all | solution.py:176
  57.4 0.4 convolution_convert_fusion.1
  58.1 1.9 %convolution_convert_fusion = bf16[64,3584]{1,0:T(8,128)(2,1)S(1)} fusion(bf16[256,3584]{1,0:T(8,128)(2,1)} %param.24, f32[64,256]{1,0:T(8,128)S(1)} %get-tuple-element.8, f32[256]{0:T(256)S(1)} %copy-done.9), kind=kOutput, calls=%fused_computation | convolution fusion | flops 117702656 | bytes 2360320 | tf_op jit(solution)/shard_map/dot_general | solution.py:220
  60.0 1.0 concatenate.9
  61.4 4.5 %concatenate.10 = bf16[32,2,7296]{2,1,0:T(2,128)(2,1)S(1)} concatenate(bf16[32,2,3584]{2,1,0:T(2,128)(2,1)S(1)} %concatenate.8, bf16[32,2,3584]{2,1,0:T(2,128)(2,1)} %concatenate.9, bf16[32,2,1]{2,1,0:T(2,128)(2,1)S(1)} %copy.28, bf16[32,2,1]{2,1,0:T(2,128)(2,1)S(1)} %copy.29, bf16[32,2,126]{2,1,0:T(2,128)(2,1)S(1)} %broadcast_in_dim.10), dimensions={2} | concatenate | bytes 1867776 | tf_op jit(solution)/shard_map/concatenate | solution.py:222
  65.9 26.5 %all_to_all.33 = bf16[32,2,7296]{2,1,0:T(2,128)(2,1)S(1)} all-to-all(bf16[32,2,7296]{2,1,0:T(2,128)(2,1)S(1)} %concatenate.10), channel_id=1, replica_groups=mesh['dp'=32,'ctx'=4,'side'=2] {'dp'}, dimensions={0} | all-to-all | bytes 1867776 | tf_op jit(solution)/shard_map/all_to_all | solution.py:223
  92.5 0.8 convert_reduce_fusion
  93.8 19.7 %all_to_all.34 = bf16[32,2,3584]{2,1,0:T(2,128)(2,1)S(1)} all-to-all(bf16[32,2,3584]{2,1,0:T(2,128)(2,1)S(1)} %broadcast_in_dim.11), channel_id=1, replica_groups=mesh['dp'=32,'ctx'=4,'side'=2] {'dp'}, dimensions={0} | all-to-all | bytes 917504 | tf_op jit(solution)/shard_map/all_to_all | solution.py:176
  113.7 2.5 %fusion = f32[8,8,256]{2,1,0:T(8,128)} fusion(bf16[8,8,3584]{2,1,0:T(8,128)(2,1)S(1)} %dot_general.17, bf16[3584,256]{1,0:T(8,128)(2,1)} %param.25), kind=kOutput, calls=%fused_computation.3 | convolution fusion | flops 117440512 | bytes 2359296 | tf_op jit(solution)/shard_map/dot_general | solution.py:233
  116.2 7.4 %all-to-all-start.5 = ((f32[8,8,256]{2,1,0:T(8,128)}), f32[8,8,256]{2,1,0:T(8,128)S(1)}, u32[]{:S(2)}, u32[]{:S(2)}) async-start(f32[8,8,256]{2,1,0:T(8,128)} %fusion), calls=%async_computation.5 | async-start | bytes 131072 | tf_op jit(solution)/shard_map/all_to_all | solution.py:235
  123.7 4.9 %all-to-all-done.5 = f32[8,8,256]{2,1,0:T(8,128)S(1)} async-done(((f32[8,8,256]{2,1,0:T(8,128)}), f32[8,8,256]{2,1,0:T(8,128)S(1)}, u32[]{:S(2)}, u32[]{:S(2)}) %all-to-all-start.5) | async-done | bytes 65568 | tf_op jit(solution)/shard_map/all_to_all | solution.py:235
  128.6 0.6 add_convert_fusion.1
  (31 shorter events, 1.8 us)
Async XLA Ops:
  0.0 57.4 %copy-start = (bf16[256,3584]{1,0:T(8,128)(2,1)S(1)}, bf16[256,3584]{1,0:T(8,128)(2,1)}, u32[]{:S(2)}) copy-start(bf16[256,3584]{1,0:T(8,128)(2,1)} %param.23) | copy-start | bytes 5505028
  0.9 1.9 %copy-start.1 = (bf16[24,64,1024]{2,1,0:T(8,128)(2,1)S(1)}, bf16[24,64,1024]{2,1,0:T(8,128)(2,1)}, u32[]{:S(2)}) copy-start(bf16[24,64,1024]{2,1,0:T(8,128)(2,1)} %param.16) | copy-start | bytes 9437188
  2.8 1.9 %copy-start.2 = (bf16[24,64,1024]{2,1,0:T(8,128)(2,1)S(1)}, bf16[24,64,1024]{2,1,0:T(8,128)(2,1)}, u32[]{:S(2)}) copy-start(bf16[24,64,1024]{2,1,0:T(8,128)(2,1)} %param.17) | copy-start | bytes 9437188
  4.7 0.7 copy-start.3
  5.4 0.7 copy-start.4
  6.1 0.7 copy-start.5
  6.7 0.7 copy-start.6
  7.4 38.4 %copy-start.7 = (bf16[1024,256]{1,0:T(8,128)(2,1)S(1)}, bf16[1024,256]{1,0:T(8,128)(2,1)}, u32[]{:S(2)}) copy-start(bf16[1024,256]{1,0:T(8,128)(2,1)} %param.21) | copy-start | bytes 1572868
  11.8 45.5 %copy-start.8 = (bf16[64,256]{1,0:T(8,128)(2,1)S(1)}, bf16[64,256]{1,0:T(8,128)(2,1)}, u32[]{:S(2)}) copy-start(bf16[64,256]{1,0:T(8,128)(2,1)} %param.20) | copy-start | bytes 98308
  11.8 45.6 %copy-start.9 = (f32[256]{0:T(256)S(1)}, f32[256]{0:T(256)}, u32[]{:S(2)}) copy-start(f32[256]{0:T(256)} %param.22) | copy-start | bytes 3076
  116.2 12.3 %all-to-all-start.5 = ((f32[8,8,256]{2,1,0:T(8,128)}), f32[8,8,256]{2,1,0:T(8,128)S(1)}, u32[]{:S(2)}, u32[]{:S(2)}) async-start(f32[8,8,256]{2,1,0:T(8,128)} %fusion), calls=%async_computation.5 | async-start | bytes 131072 | tf_op jit(solution)/shard_map/all_to_all | solution.py:235

commit v2 on v1

v2 whole, which is shorter than its diff:
```python
import math

import jax
import jax.numpy as jnp
from jax import lax
from jax.experimental import pallas as pl
from jax.experimental.pallas import tpu as pltpu
from jax.sharding import Mesh
from jax.sharding import PartitionSpec as P

D = 8192
KVH = 8
HD = 128
PAGE = 64
PMAX = 12
G = 8
ROWS_DEV = 2
SLOTS = ROWS_DEV * PMAX
TOKENS = SLOTS * PAGE
QROWS = ROWS_DEV * KVH * G
CHUNKS = 4
CHUNK = TOKENS // CHUNKS
NEG = -1e30
SHARD_AXES = ("ctx", "side")
DP_AXES = ("z2", "z1", "z0", "y1", "y0")
SUM_AXES = ("y1", "y0", "z2", "z1", "z0")
WIDE_STEPS = 7
ATTEND_VMEM = 64 * 1024 * 1024

norm_eps = 1e-05
f32 = jnp.float32
bf16 = jnp.bfloat16


def attend_kernel(
    table_hbm, lengths_hbm, q_hbm, nk_hbm, nv_hbm, key_hbm, value_hbm, out_ref,
    table, lengths, q_two, nk_ref, nv_ref, q_rows, keys, values, q_wide, scores, owner,
    small_sem, key_sem, value_sem,
):
    shard = lax.axis_index(SHARD_AXES)
    small = [
        pltpu.make_async_copy(src, dst, small_sem.at[i])
        for i, (src, dst) in enumerate(
            [(q_hbm, q_two), (nk_hbm, nk_ref), (nv_hbm, nv_ref), (table_hbm, table), (lengths_hbm, lengths)]
        )
    ]
    for one in small:
        one.start()

    def copy(src, dst, sem, c):
        rows = pl.ds(c * CHUNK, CHUNK)
        return pltpu.make_async_copy(src.at[rows], dst.at[rows], sem.at[c])

    for c in range(CHUNKS):
        copy(key_hbm, keys, key_sem, c).start()
    for c in range(CHUNKS):
        copy(value_hbm, values, value_sem, c).start()

    for one in small:
        one.wait()

    for k in range(SLOTS):
        owner[table[0, 0, k]] = k

    def limit_of(slot, row):
        k = owner[slot]
        own = lax.div(k, PMAX)
        page = lax.rem(k, PMAX)
        start = (page * 8 + shard) * PAGE
        count = lengths[row] - start
        return jnp.where(own == row, count, 0)

    q_all = q_two[...].astype(f32)
    for n in range(KVH * G):
        for r in range(ROWS_DEV):
            at = r * KVH * G + n
            q_rows[at : at + 1, :] = q_all[r : r + 1, n * HD : (n + 1) * HD]
    q = q_rows[...].astype(bf16)
    head_of_row = lax.rem(lax.div(lax.broadcasted_iota(jnp.int32, (QROWS, HD), 0), G), KVH)
    for h in range(KVH):
        q_wide[:, h * HD : (h + 1) * HD] = jnp.where(head_of_row == h, q, jnp.zeros_like(q))

    scale = 1.0 / math.sqrt(HD)

    def per_group(ref):
        parts = []
        for r in range(ROWS_DEV):
            for h in range(KVH):
                one = ref[r : r + 1, h * HD : (h + 1) * HD].astype(f32)
                parts.append(jnp.broadcast_to(one, (G, HD)))
        return jnp.concatenate(parts, axis=0)

    fresh = jnp.sum(q.astype(f32) * per_group(nk_ref), axis=1, keepdims=True) * scale
    fresh = jnp.where(shard == 0, fresh, NEG)
    new_values = per_group(nv_ref)

    lane = lax.broadcasted_iota(jnp.int32, (QROWS // ROWS_DEV, HD), 1)
    within = lax.rem(lane, PAGE)
    first_half = lane < PAGE
    peak = fresh
    for c in range(CHUNKS):
        copy(key_hbm, keys, key_sem, c).wait()
        part = lax.dot_general(
            q_wide[...], keys[c * CHUNK : (c + 1) * CHUNK, :],
            (((1,), (1,)), ((), ())), preferred_element_type=f32,
        ) * scale
        for t in range(CHUNK // HD):
            slot = (c * CHUNK + t * HD) // PAGE
            tiles = []
            for r in range(ROWS_DEV):
                live = within < jnp.where(first_half, limit_of(slot, r), limit_of(slot + 1, r))
                tile = part[r * KVH * G : (r + 1) * KVH * G, t * HD : (t + 1) * HD]
                tiles.append(jnp.where(live, tile, NEG))
            tile = jnp.concatenate(tiles, axis=0)
            scores[:, c * CHUNK + t * HD : c * CHUNK + (t + 1) * HD] = tile
            peak = jnp.maximum(peak, jnp.max(tile, axis=1, keepdims=True))

    total = jnp.zeros((QROWS, HD), f32)
    mixed = jnp.zeros((QROWS, KVH * HD), f32)
    for c in range(CHUNKS):
        part = scores[:, c * CHUNK : (c + 1) * CHUNK]
        weight = jnp.where(part > 0.5 * NEG, jnp.exp(part - peak), 0.0)
        for t in range(CHUNK // HD):
            total = total + weight[:, t * HD : (t + 1) * HD]
        copy(value_hbm, values, value_sem, c).wait()
        mixed = mixed + jnp.dot(
            weight.astype(bf16), values[c * CHUNK : (c + 1) * CHUNK, :], preferred_element_type=f32
        )
    fresh_weight = jnp.where(shard == 0, jnp.exp(fresh - peak), 0.0)
    total = jnp.sum(total, axis=1, keepdims=True) + fresh_weight
    added = fresh_weight * new_values
    stat_lane = lax.broadcasted_iota(jnp.int32, (QROWS, HD), 1)
    stats = jnp.where(stat_lane == 0, peak, total)
    for h in range(KVH):
        for r in range(ROWS_DEV):
            at = (r * KVH + h) * G
            own = mixed[at : at + G, h * HD : (h + 1) * HD] + added[at : at + G, :]
            out_ref[h, r * G : (r + 1) * G, 0:HD] = own
            out_ref[h, r * G : (r + 1) * G, HD : 2 * HD] = stats[at : at + G, :]


def attend(table, lengths, q, new_key, new_value, keys, values):
    vmem = pl.BlockSpec(memory_space=pltpu.VMEM)
    hbm = pl.BlockSpec(memory_space=pltpu.HBM)
    return pl.pallas_call(
        attend_kernel,
        out_shape=jax.ShapeDtypeStruct((KVH, ROWS_DEV * G, 2 * HD), f32),
        in_specs=[hbm] * 7,
        out_specs=vmem,
        scratch_shapes=[
            pltpu.SMEM((1, 1, SLOTS), jnp.int32),
            pltpu.SMEM((ROWS_DEV,), jnp.int32),
            pltpu.VMEM((ROWS_DEV, KVH * G * HD), bf16),
            pltpu.VMEM((ROWS_DEV, KVH * HD), bf16),
            pltpu.VMEM((ROWS_DEV, KVH * HD), bf16),
            pltpu.VMEM((QROWS, HD), f32),
            pltpu.VMEM((TOKENS, KVH * HD), bf16),
            pltpu.VMEM((TOKENS, KVH * HD), bf16),
            pltpu.VMEM((QROWS, KVH * HD), bf16),
            pltpu.VMEM((QROWS, TOKENS), f32),
            pltpu.SMEM((SLOTS,), jnp.int32),
            pltpu.SemaphoreType.DMA((5,)),
            pltpu.SemaphoreType.DMA((CHUNKS,)),
            pltpu.SemaphoreType.DMA((CHUNKS,)),
        ],
        compiler_params=pltpu.CompilerParams(vmem_limit_bytes=ATTEND_VMEM),
        name="attend",
    )(table, lengths, q, new_key, new_value, keys, values)


def merge_kernel(parts_ref, out_ref):
    shards = parts_ref.shape[0]
    peak = parts_ref[0, :, HD : HD + 1]
    for s in range(1, shards):
        peak = jnp.maximum(peak, parts_ref[s, :, HD : HD + 1])
    total = jnp.zeros_like(peak)
    mixed = jnp.zeros((ROWS_DEV * G, HD), f32)
    for s in range(shards):
        factor = jnp.exp(parts_ref[s, :, HD : HD + 1] - peak)
        total = total + factor * parts_ref[s, :, HD + 1 : HD + 2]
        mixed = mixed + factor * parts_ref[s, :, 0:HD]
    attended = (mixed / total).astype(bf16)
    for i in range(out_ref.shape[0]):
        out_ref[i] = attended


def merge(parts, copies):
    vmem = pl.BlockSpec(memory_space=pltpu.VMEM)
    return pl.pallas_call(
        merge_kernel,
        out_shape=jax.ShapeDtypeStruct((copies, ROWS_DEV * G, HD), bf16),
        in_specs=[vmem],
        out_specs=vmem,
        compiler_params=pltpu.CompilerParams(vmem_limit_bytes=4 * 1024 * 1024),
        cost_estimate=pl.CostEstimate(flops=20_000_000_000, bytes_accessed=0, transcendentals=0),
        name="merge",
    )(parts)


def project_kernel(attended_ref, weight_ref, out_ref, rows_ref):
    groups = attended_ref.shape[0]
    for n in range(groups):
        rows_ref[n * ROWS_DEV * G : (n + 1) * ROWS_DEV * G, :] = attended_ref[n].astype(f32)
    heads = [rows_ref[pl.ds(g, groups * ROWS_DEV, stride=G), :] for g in range(G)]
    wide = jnp.concatenate(heads, axis=1).astype(bf16)
    result = jnp.dot(wide, weight_ref[...], preferred_element_type=f32).astype(bf16)
    for i in range(out_ref.shape[0]):
        out_ref[i] = result


def project(attended, weight, copies):
    groups = attended.shape[0]
    vmem = pl.BlockSpec(memory_space=pltpu.VMEM)
    return pl.pallas_call(
        project_kernel,
        out_shape=jax.ShapeDtypeStruct((copies, groups * ROWS_DEV, weight.shape[1]), bf16),
        in_specs=[vmem, vmem],
        out_specs=vmem,
        scratch_shapes=[pltpu.VMEM((groups * ROWS_DEV * G, HD), f32)],
        compiler_params=pltpu.CompilerParams(vmem_limit_bytes=8 * 1024 * 1024),
        cost_estimate=pl.CostEstimate(flops=20_000_000_000, bytes_accessed=0, transcendentals=0),
        name="project",
    )(attended, weight)


def widen_kernel(came_ref, residual_ref, gain_ref, gate_ref, up_ref, sent_ref, middle_ref):
    hidden_here = gate_ref.shape[1]
    step = hidden_here // WIDE_STEPS
    projected = came_ref[0].astype(f32)
    for s in range(1, came_ref.shape[0]):
        projected = projected + came_ref[s].astype(f32)
    middle = (residual_ref[...].astype(f32) + projected).astype(bf16)
    middle_ref[...] = middle
    middle_f = middle.astype(f32)
    scaled = (middle_f * gain_ref[...]).astype(bf16)
    squares = jnp.sum(middle_f * middle_f, axis=1, keepdims=True)
    high = squares.astype(bf16).astype(f32)
    lane = lax.broadcasted_iota(jnp.int32, (middle.shape[0], HD), 1)
    tail = jnp.where(lane == 0, high, jnp.where(lane == 1, squares - high, 0.0))
    sent_ref[:, 2 * hidden_here :] = tail.astype(bf16)
    for n, weight_ref in enumerate((gate_ref, up_ref)):
        for c in range(WIDE_STEPS):
            at = n * hidden_here + c * step
            sent_ref[:, at : at + step] = jnp.dot(
                scaled, weight_ref[:, c * step : (c + 1) * step], preferred_element_type=f32
            ).astype(bf16)


def widen(came, residual, gain, gate_weight, up_weight):
    rows, width = residual.shape
    hidden_here = gate_weight.shape[1]
    vmem = pl.BlockSpec(memory_space=pltpu.VMEM)
    return pl.pallas_call(
        widen_kernel,
        out_shape=(
            jax.ShapeDtypeStruct((rows, 2 * hidden_here + HD), bf16),
            jax.ShapeDtypeStruct((rows, width), bf16),
        ),
        in_specs=[vmem] * 5,
        out_specs=(vmem, vmem),
        compiler_params=pltpu.CompilerParams(vmem_limit_bytes=8 * 1024 * 1024),
        name="widen",
    )(came, residual, gain, gate_weight, up_weight)


def narrow_kernel(hidden_ref, down_ref, out_ref):
    out_ref[...] = jnp.dot(hidden_ref[...], down_ref[...], preferred_element_type=f32)


def narrow(hidden, down_weight):
    vmem = pl.BlockSpec(memory_space=pltpu.VMEM)
    return pl.pallas_call(
        narrow_kernel,
        out_shape=jax.ShapeDtypeStruct((hidden.shape[0], down_weight.shape[1]), f32),
        in_specs=[vmem, vmem],
        out_specs=vmem,
        compiler_params=pltpu.CompilerParams(vmem_limit_bytes=8 * 1024 * 1024),
        name="narrow",
    )(hidden, down_weight)


def copies_for(x, axes):
    return jnp.broadcast_to(x[None], (lax.axis_size(axes),) + x.shape)


def body(
    queries,
    new_key,
    new_value,
    key_pool,
    value_pool,
    page_table,
    lengths,
    residual,
    out_weight,
    norm_gain,
    gate_weight,
    up_weight,
    down_weight,
):
    shards = lax.axis_size(SHARD_AXES)
    shard_index = lax.axis_index(SHARD_AXES)
    rows, width = residual.shape
    hidden_here = gate_weight.shape[1]

    parts = attend(
        page_table,
        lengths,
        queries,
        new_key,
        new_value,
        key_pool.reshape(TOKENS, KVH * HD),
        value_pool.reshape(TOKENS, KVH * HD),
    )
    attended = merge(lax.all_to_all(parts, SHARD_AXES, 0, 0), lax.axis_size(DP_AXES))
    attended = lax.all_to_all(attended, DP_AXES, 0, 0)
    partial_proj = project(attended, out_weight, shards)
    came = lax.all_to_all(partial_proj, SHARD_AXES, 0, 0)
    sent, middle = widen(came, residual, norm_gain.reshape(1, width), gate_weight, up_weight)
    near, far = SUM_AXES[:2], SUM_AXES[2:]
    spread = lax.axis_size(near)
    came = lax.all_to_all(sent.reshape(spread, rows // spread, sent.shape[1]), near, 0, 0)
    sent = jnp.sum(came.astype(f32), axis=0).astype(bf16)
    came = lax.all_to_all(sent.reshape(lax.axis_size(far), ROWS_DEV, sent.shape[1]), far, 0, 0)
    sums = jnp.sum(came.astype(f32), axis=0)
    square_sum = sums[:, 2 * hidden_here] + sums[:, 2 * hidden_here + 1]
    inverse = (1.0 / jnp.sqrt(square_sum / D + norm_eps))[:, None]
    gate = sums[:, :hidden_here] * inverse
    up = sums[:, hidden_here : 2 * hidden_here] * inverse
    hidden = (jax.nn.silu(gate) * up).astype(bf16)
    hidden = lax.all_to_all(copies_for(hidden, SUM_AXES), SUM_AXES, 0, 0)
    down = narrow(hidden.reshape(rows, hidden_here), down_weight)
    share_rows = rows // shards
    down = lax.all_to_all(down.reshape(shards, share_rows, width), SHARD_AXES, 0, 0)
    middle_own = lax.dynamic_slice_in_dim(middle, shard_index * share_rows, share_rows, 0)
    return (middle_own.astype(f32) + jnp.sum(down, axis=0)).astype(bf16)


def solution(mesh):
    lines, cores = mesh.shape["ctx"], mesh.shape["side"]
    split = Mesh(
        mesh.devices.reshape((2,) * len(DP_AXES) + (lines, cores)), DP_AXES + SHARD_AXES
    )
    dp, block = DP_AXES, SHARD_AXES
    placed = (
        P(dp, None),
        P(dp, None),
        P(dp, None),
        P(dp + block, None, None),
        P(dp + block, None, None),
        P(dp, block, None),
        P(dp),
        P(None, dp),
        P(block, dp),
        P(dp),
        P(dp, block),
        P(dp, block),
        P(block, dp),
    )
    return jax.shard_map(
        body, mesh=split, in_specs=placed, out_specs=P(block, dp), check_vma=False
    )
```

time: 130 us -> 107 us (0.82)
  local copies, waits for them, and re-layouts: 14.7 us -> 0.53 us
  blocking collectives: 89 us -> 83.4 us
  matrix products: 5.14 us -> 0 us
  starting transfers between devices: 7.44 us -> 8.96 us
  Pallas kernels: 6.05 us -> 7.53 us
    unnamed x20 -> x12, local copies, waits for them, and re-layouts: 6.47 us -> 0.03 us
    concatenate x3 -> x0, local copies, waits for them, and re-layouts: 5.67 us -> none  [body(): jnp.concatenate([gate_part, up_part, squares_high, squares_low, pad], axi...]
    all_to_all x5 -> x6, blocking collectives: 89 us -> 83.4 us  [the longest x1 19.7 us: body(): attended = lax.all_to_all(attended, DP_AXES, 0, 0)]
    dot_general x4 -> x0, matrix products: 5.14 us -> none  [the longest x1 2.54 us: body(): down = jnp.dot(hidden, down_weight, preferred_element_type=f32)]
    all_to_all x1, starting transfers between devices: 7.44 us -> 8.96 us  [body(): lax.all_to_all(down.reshape(shards, share_rows, width), SHARD_AXES, 0, 0)]
where the time goes in v2:
time: 107 us
  blocking collectives  83.4 us (78%)
  starting transfers between devices  8.96 us (8%)
  Pallas kernels  7.53 us (7%)
  waiting for transfers between devices  4.85 us (5%)
  other arithmetic  1.33 us (1%)
    all_to_all x1, blocking collectives, body(): attended = lax.all_to_all(attended, DP_AXES, 0, 0)  19.7 us
    all_to_all x1, blocking collectives, body(): lax.all_to_all(sent.reshape(spread, rows // spread, sent.shape[1]), near,...  15.2 us
    all_to_all x1, blocking collectives, body(): hidden = lax.all_to_all(copies_for(hidden, SUM_AXES), SUM_AXES, 0, 0)  13.8 us
    all_to_all x1, blocking collectives, body(): lax.all_to_all(parts, SHARD_AXES, 0, 0)  11.8 us
    all_to_all x1, blocking collectives, body(): came = lax.all_to_all(partial_proj, SHARD_AXES, 0, 0)  11.5 us
    all_to_all x1, blocking collectives, body(): lax.all_to_all(sent.reshape(lax.axis_size(far), ROWS_DEV, sent.shape[1]),...  11.5 us
    all_to_all x1, starting transfers between devices, body(): lax.all_to_all(down.reshape(shards, share_rows, width), SHARD_AXES, 0, 0)  8.96 us
    pallas_call x1, Pallas kernels, attend(): pl.pallas_call(attend_kernel, out_shape=jax.ShapeDtypeStruct((KVH, ROWS_D...  5.32 us
  transfers between devices with their start and end apart: 1, of which 1 were waited for; matrix products, arithmetic and copies ran while one was open for 0% of the time, Pallas kernels for 0%

profile of v2, /device:TPU:1, one launch (start us, length us, event | category | flops | bytes accessed | tf_op | source)
XLA Modules:
  0.0 106.7 jit_solution(6205856501837774454)
XLA Ops:
  0.0 5.3 %attend.1 = f32[8,16,256]{2,1,0:T(8,128)} custom-call(s32[1,1,24]{2,1,0:T(1,128)} %table_hbm.1, s32[2]{0:T(128)} %lengths_hbm.1, bf16[2,8192]{1,0:T(2,128)(2,1)} %q_hbm.1, bf16[2,1024]{1,0:T(2,128)(2,1)} %nk_hbm.1, bf16[2,1024]{1,0:T(2,128)(2,1)} %nv_hbm.1, bf16[1536,1024]{1,0:T(8,128)(2,1)} %bitcast.7, bf16[1536,1024]{1,0:T(8,128)(2,1)} %bitcast.8), custom_call_target="tpu_custom_call" | custom-call | tf_op jit(solution)/shard_map/attend/pallas_call | solution.py:145
  5.3 11.8 %all_to_all.35.parts_ref = f32[8,16,256]{2,1,0:T(8,128)S(1)} all-to-all(f32[8,16,256]{2,1,0:T(8,128)} %attend.1), channel_id=1, replica_groups=mesh['z2'=2,'z1'=2,'z0'=2,'y1'=2,'y0'=2,'ctx'=4,'side'=2] {'ctx','side'}, dimensions={0} | all-to-all | bytes 262144 | tf_op jit(solution)/shard_map/all_to_all | solution.py:315
  17.1 0.2 merge.1
  17.3 19.7 %all_to_all.36.attended_ref = bf16[32,16,128]{2,1,0:T(8,128)(2,1)S(1)} all-to-all(bf16[32,16,128]{2,1,0:T(8,128)(2,1)S(1)} %merge.1), channel_id=1, replica_groups=mesh['z2'=2,'z1'=2,'z0'=2,'y1'=2,'y0'=2,'ctx'=4,'side'=2] {'z2','z1','z0..., dimensions={0} | all-to-all | bytes 262144 | tf_op jit(solution)/shard_map/all_to_all | solution.py:316
  37.0 0.0 copy-start.4
  37.0 0.2 project.1
  37.2 11.5 %all_to_all.37.came_ref = bf16[8,64,256]{2,1,0:T(8,128)(2,1)S(1)} all-to-all(bf16[8,64,256]{2,1,0:T(8,128)(2,1)S(1)} %project.1), channel_id=1, replica_groups=mesh['z2'=2,'z1'=2,'z0'=2,'y1'=2,'y0'=2,'ctx'=4,'side'=2] {'ctx','side'}, dimensions={0} | all-to-all | bytes 524288 | tf_op jit(solution)/shard_map/all_to_all | solution.py:318
  48.7 0.0 copy-done
  48.7 0.0 copy-done.3
  48.7 0.8 widen.1
  49.5 15.2 %all_to_all.38 = bf16[4,16,7296]{2,1,0:T(8,128)(2,1)S(1)} all-to-all(bf16[4,16,7296]{2,1,0:T(8,128)(2,1)S(1)} %bitcast.5), channel_id=1, replica_groups=mesh['z2'=2,'z1'=2,'z0'=2,'y1'=2,'y0'=2,'ctx'=4,'side'=2] {'y1','y0'}, dimensions={0} | all-to-all | bytes 1867776 | tf_op jit(solution)/shard_map/all_to_all | solution.py:322
  64.7 0.2 reduce_sum.30
  64.9 0.1 reshape.26
  65.0 11.5 %all_to_all.39 = bf16[8,2,7296]{2,1,0:T(2,128)(2,1)S(1)} all-to-all(bf16[8,2,7296]{2,1,0:T(2,128)(2,1)S(1)} %reshape.26), channel_id=1, replica_groups=mesh['z2'=2,'z1'=2,'z0'=2,'y1'=2,'y0'=2,'ctx'=4,'side'=2] {'z2','z1','z0'}, dimensions={0} | all-to-all | bytes 466944 | tf_op jit(solution)/shard_map/all_to_all | solution.py:324
  76.5 0.2 convert_reduce_fusion
  76.6 0.2 fusion.5
  76.8 0.1 fusion.1
  77.0 0.2 broadcast_in_dim.2
  77.2 13.8 %all_to_all.40 = bf16[32,2,3584]{2,1,0:T(2,128)(2,1)S(1)} all-to-all(bf16[32,2,3584]{2,1,0:T(2,128)(2,1)S(1)} %broadcast_in_dim.2), channel_id=1, replica_groups=mesh['z2'=2,'z1'=2,'z0'=2,'y1'=2,'y0'=2,'ctx'=4,'side'=2] {'y1','y0','z2..., dimensions={0} | all-to-all | bytes 917504 | tf_op jit(solution)/shard_map/all_to_all | solution.py:331
  91.0 0.2 reshape.27.hidden_ref
  91.2 1.1 narrow.1
  92.3 9.0 %all-to-all-start.6 = ((f32[8,8,256]{2,1,0:T(8,128)}), f32[8,8,256]{2,1,0:T(8,128)S(1)}, u32[]{:S(2)}, u32[]{:S(2)}) async-start(f32[8,8,256]{2,1,0:T(8,128)} %bitcast.4), calls=%async_computation.6 | async-start | bytes 131072 | tf_op jit(solution)/shard_map/all_to_all | solution.py:334
  101.2 4.9 %all-to-all-done.6 = f32[8,8,256]{2,1,0:T(8,128)S(1)} async-done(((f32[8,8,256]{2,1,0:T(8,128)}), f32[8,8,256]{2,1,0:T(8,128)S(1)}, u32[]{:S(2)}, u32[]{:S(2)}) %all-to-all-start.6) | async-done | bytes 65568 | tf_op jit(solution)/shard_map/all_to_all | solution.py:334
  106.1 0.6 add_convert_fusion
  (10 shorter events, 0.0 us)
Async XLA Ops:
  17.1 19.8 %copy-start.5 = (bf16[1024,256]{1,0:T(8,128)(2,1)S(1)}, bf16[1024,256]{1,0:T(8,128)(2,1)}, u32[]{:S(2)}) copy-start(bf16[1024,256]{1,0:T(8,128)(2,1)} %weight_ref.1) | copy-start | bytes 1572868
  37.0 11.7 %copy-start = (bf16[256,3584]{1,0:T(8,128)(2,1)S(1)}, bf16[256,3584]{1,0:T(8,128)(2,1)}, u32[]{:S(2)}) copy-start(bf16[256,3584]{1,0:T(8,128)(2,1)} %gate_ref.1) | copy-start | bytes 5505028
  37.0 11.7 %copy-start.1 = (bf16[256,3584]{1,0:T(8,128)(2,1)S(1)}, bf16[256,3584]{1,0:T(8,128)(2,1)}, u32[]{:S(2)}) copy-start(bf16[256,3584]{1,0:T(8,128)(2,1)} %up_ref.1) | copy-start | bytes 5505028
  37.0 11.7 %copy-start.3 = (bf16[64,256]{1,0:T(8,128)(2,1)S(1)}, bf16[64,256]{1,0:T(8,128)(2,1)}, u32[]{:S(2)}) copy-start(bf16[64,256]{1,0:T(8,128)(2,1)} %residual_ref.1) | copy-start | bytes 98308
  37.0 11.7 %copy-start.4 = (f32[256]{0:T(256)S(1)}, f32[256]{0:T(256)}, u32[]{:S(2)}) copy-start(f32[256]{0:T(256)} %param.22) | copy-start | bytes 3076
  64.9 26.3 %copy-start.2 = (bf16[3584,256]{1,0:T(8,128)(2,1)S(1)}, bf16[3584,256]{1,0:T(8,128)(2,1)}, u32[]{:S(2)}) copy-start(bf16[3584,256]{1,0:T(8,128)(2,1)} %down_ref.1) | copy-start | bytes 5505028
  92.3 13.8 %all-to-all-start.6 = ((f32[8,8,256]{2,1,0:T(8,128)}), f32[8,8,256]{2,1,0:T(8,128)S(1)}, u32[]{:S(2)}, u32[]{:S(2)}) async-start(f32[8,8,256]{2,1,0:T(8,128)} %bitcast.4), calls=%async_computation.6 | async-start | bytes 131072 | tf_op jit(solution)/shard_map/all_to_all | solution.py:334

commit v3 on v2

--- a/solution.py
+++ b/solution.py
@@ -23,8 +23,9 @@
 NEG = -1e30
 SHARD_AXES = ("ctx", "side")
 DP_AXES = ("z2", "z1", "z0", "y1", "y0")
-SUM_AXES = ("y1", "y0", "z2", "z1", "z0")
-WIDE_STEPS = 7
+NEAR_AXES = ("y1", "y0", "z0")
+FAR_AXES = ("z2", "z1")
+SPREAD_Y = 4
 ATTEND_VMEM = 64 * 1024 * 1024
 
 norm_eps = 1e-05
@@ -223,64 +224,107 @@
     )(attended, weight)
 
 
-def widen_kernel(came_ref, residual_ref, gain_ref, gate_ref, up_ref, sent_ref, middle_ref):
-    hidden_here = gate_ref.shape[1]
-    step = hidden_here // WIDE_STEPS
+def widen_kernel(
+    came_ref, residual_ref, gain_ref, gate_ref, up_ref, sent_ref, own_ref, middle_ref
+):
     projected = came_ref[0].astype(f32)
     for s in range(1, came_ref.shape[0]):
         projected = projected + came_ref[s].astype(f32)
-    middle = (residual_ref[...].astype(f32) + projected).astype(bf16)
+    middle = (residual_ref[...].astype(f32) + projected).astype(bf16).astype(f32)
     middle_ref[...] = middle
-    middle_f = middle.astype(f32)
-    scaled = (middle_f * gain_ref[...]).astype(bf16)
-    squares = jnp.sum(middle_f * middle_f, axis=1, keepdims=True)
+    share = own_ref.shape[0]
+    at = pl.multiple_of(lax.axis_index(SHARD_AXES) * share, share)
+    own_ref[...] = middle_ref[pl.ds(at, share), :]
+    scaled = (middle * gain_ref[...]).astype(bf16)
+    squares = jnp.sum(middle * middle, axis=1, keepdims=True)
     high = squares.astype(bf16).astype(f32)
     lane = lax.broadcasted_iota(jnp.int32, (middle.shape[0], HD), 1)
-    tail = jnp.where(lane == 0, high, jnp.where(lane == 1, squares - high, 0.0))
-    sent_ref[:, 2 * hidden_here :] = tail.astype(bf16)
-    for n, weight_ref in enumerate((gate_ref, up_ref)):
-        for c in range(WIDE_STEPS):
-            at = n * hidden_here + c * step
-            sent_ref[:, at : at + step] = jnp.dot(
-                scaled, weight_ref[:, c * step : (c + 1) * step], preferred_element_type=f32
+    tail = jnp.where(lane == 0, high, jnp.where(lane == 1, squares - high, 0.0)).astype(bf16)
+    blocks = sent_ref.shape[0]
+    units = gate_ref.shape[1] // blocks
+    for b in range(blocks):
+        for n, weight_ref in enumerate((gate_ref, up_ref)):
+            sent_ref[b, :, n * units : (n + 1) * units] = jnp.dot(
+                scaled, weight_ref[:, b * units : (b + 1) * units], preferred_element_type=f32
             ).astype(bf16)
-
-
-def widen(came, residual, gain, gate_weight, up_weight):
+        sent_ref[b, :, 2 * units :] = tail
+
+
+def widen(came, residual, gain, gate_weight, up_weight, blocks, share):
     rows, width = residual.shape
-    hidden_here = gate_weight.shape[1]
+    units = gate_weight.shape[1] // blocks
     vmem = pl.BlockSpec(memory_space=pltpu.VMEM)
     return pl.pallas_call(
         widen_kernel,
         out_shape=(
-            jax.ShapeDtypeStruct((rows, 2 * hidden_here + HD), bf16),
-            jax.ShapeDtypeStruct((rows, width), bf16),
+            jax.ShapeDtypeStruct((blocks, rows, 2 * units + HD), bf16),
+            jax.ShapeDtypeStruct((share, width), f32),
         ),
         in_specs=[vmem] * 5,
         out_specs=(vmem, vmem),
+        scratch_shapes=[pltpu.VMEM((rows, width), f32)],
         compiler_params=pltpu.CompilerParams(vmem_limit_bytes=8 * 1024 * 1024),
         name="widen",
     )(came, residual, gain, gate_weight, up_weight)
 
 
-def narrow_kernel(hidden_ref, down_ref, out_ref):
-    out_ref[...] = jnp.dot(hidden_ref[...], down_ref[...], preferred_element_type=f32)
+def finish_kernel(came_ref, out_ref):
+    units = out_ref.shape[2]
+    sums = came_ref[0].astype(f32)
+    for n in range(1, came_ref.shape[0]):
+        sums = sums + came_ref[n].astype(f32)
+    squares = sums[:, 2 * units : 2 * units + 1] + sums[:, 2 * units + 1 : 2 * units + 2]
+    inverse = 1.0 / jnp.sqrt(squares / D + norm_eps)
+    gate = sums[:, :units] * inverse
+    up = sums[:, units : 2 * units] * inverse
+    hidden = (gate / (1.0 + jnp.exp(-gate)) * up).astype(bf16)
+    for n in range(out_ref.shape[0]):
+        out_ref[n] = hidden
+
+
+def finish(came, copies):
+    _, rows, wide = came.shape
+    vmem = pl.BlockSpec(memory_space=pltpu.VMEM)
+    return pl.pallas_call(
+        finish_kernel,
+        out_shape=jax.ShapeDtypeStruct((copies, rows, (wide - HD) // 2), bf16),
+        in_specs=[vmem],
+        out_specs=vmem,
+        compiler_params=pltpu.CompilerParams(vmem_limit_bytes=4 * 1024 * 1024),
+        name="finish",
+    )(came)
+
+
+def narrow_kernel(hidden_ref, down_ref, out_ref, rows_ref):
+    groups, rows, units = hidden_ref.shape
+    blocks = down_ref.shape[0] // units
+    total = jnp.zeros(out_ref.shape, f32)
+    for b in range(blocks):
+        for n in range(groups // blocks):
+            place = (n % 2) * (groups // blocks // 2) + n // 2
+            rows_ref[b, place * rows : (place + 1) * rows, :] = hidden_ref[n * blocks + b].astype(f32)
+        total = total + jnp.dot(
+            rows_ref[b].astype(bf16),
+            down_ref[b * units : (b + 1) * units, :],
+            preferred_element_type=f32,
+        )
+    out_ref[...] = total
 
 
 def narrow(hidden, down_weight):
+    groups, rows, units = hidden.shape
+    blocks = down_weight.shape[0] // units
+    all_rows = rows * groups // blocks
     vmem = pl.BlockSpec(memory_space=pltpu.VMEM)
     return pl.pallas_call(
         narrow_kernel,
-        out_shape=jax.ShapeDtypeStruct((hidden.shape[0], down_weight.shape[1]), f32),
+        out_shape=jax.ShapeDtypeStruct((all_rows, down_weight.shape[1]), f32),
         in_specs=[vmem, vmem],
         out_specs=vmem,
+        scratch_shapes=[pltpu.VMEM((blocks, all_rows, units), f32)],
         compiler_params=pltpu.CompilerParams(vmem_limit_bytes=8 * 1024 * 1024),
         name="narrow",
     )(hidden, down_weight)
-
-
-def copies_for(x, axes):
-    return jnp.broadcast_to(x[None], (lax.axis_size(axes),) + x.shape)
 
 
 def body(
@@ -299,9 +343,10 @@
     down_weight,
 ):
     shards = lax.axis_size(SHARD_AXES)
-    shard_index = lax.axis_index(SHARD_AXES)
+    groups = lax.axis_size(DP_AXES)
+    near, far = lax.axis_size(NEAR_AXES), lax.axis_size(FAR_AXES)
     rows, width = residual.shape
-    hidden_here = gate_weight.shape[1]
+    share_rows = rows // shards
 
     parts = attend(
         page_table,
@@ -312,28 +357,20 @@
         key_pool.reshape(TOKENS, KVH * HD),
         value_pool.reshape(TOKENS, KVH * HD),
     )
-    attended = merge(lax.all_to_all(parts, SHARD_AXES, 0, 0), lax.axis_size(DP_AXES))
+    attended = merge(lax.all_to_all(parts, SHARD_AXES, 0, 0), groups)
     attended = lax.all_to_all(attended, DP_AXES, 0, 0)
-    partial_proj = project(attended, out_weight, shards)
-    came = lax.all_to_all(partial_proj, SHARD_AXES, 0, 0)
-    sent, middle = widen(came, residual, norm_gain.reshape(1, width), gate_weight, up_weight)
-    near, far = SUM_AXES[:2], SUM_AXES[2:]
-    spread = lax.axis_size(near)
-    came = lax.all_to_all(sent.reshape(spread, rows // spread, sent.shape[1]), near, 0, 0)
+    came = lax.all_to_all(project(attended, out_weight, shards), SHARD_AXES, 0, 0)
+    sent, middle_own = widen(
+        came, residual, norm_gain.reshape(1, width), gate_weight, up_weight, SPREAD_Y, share_rows
+    )
+    half = rows * SPREAD_Y // near
+    came = lax.all_to_all(sent.reshape(near, half, sent.shape[2]), NEAR_AXES, 0, 0)
     sent = jnp.sum(came.astype(f32), axis=0).astype(bf16)
-    came = lax.all_to_all(sent.reshape(lax.axis_size(far), ROWS_DEV, sent.shape[1]), far, 0, 0)
-    sums = jnp.sum(came.astype(f32), axis=0)
-    square_sum = sums[:, 2 * hidden_here] + sums[:, 2 * hidden_here + 1]
-    inverse = (1.0 / jnp.sqrt(square_sum / D + norm_eps))[:, None]
-    gate = sums[:, :hidden_here] * inverse
-    up = sums[:, hidden_here : 2 * hidden_here] * inverse
-    hidden = (jax.nn.silu(gate) * up).astype(bf16)
-    hidden = lax.all_to_all(copies_for(hidden, SUM_AXES), SUM_AXES, 0, 0)
-    down = narrow(hidden.reshape(rows, hidden_here), down_weight)
-    share_rows = rows // shards
+    came = lax.all_to_all(sent.reshape(far, half // far, sent.shape[1]), FAR_AXES, 0, 0)
+    hidden = lax.all_to_all(finish(came, groups), DP_AXES, 0, 0)
+    down = narrow(hidden, down_weight)
     down = lax.all_to_all(down.reshape(shards, share_rows, width), SHARD_AXES, 0, 0)
-    middle_own = lax.dynamic_slice_in_dim(middle, shard_index * share_rows, share_rows, 0)
-    return (middle_own.astype(f32) + jnp.sum(down, axis=0)).astype(bf16)
+    return (middle_own + jnp.sum(down, axis=0)).astype(bf16)
 
 
 def solution(mesh):

time: 107 us -> 105 us (0.981)
  blocking collectives: 83.4 us -> 97.2 us
  starting transfers between devices: 8.96 us -> 0 us
  waiting for transfers between devices: 4.85 us -> 0 us
    all_to_all x5 -> x6, blocking collectives: 63.7 us -> 77.5 us  [the longest x1 16.2 us: body(): lax.all_to_all(sent.reshape(near, half, sent.shape[2]), NEAR_AXES, 0, 0)]
    all_to_all x1 -> x0, starting transfers between devices: 8.96 us -> none  [body(): lax.all_to_all(down.reshape(shards, share_rows, width), SHARD_AXES, 0, 0)]
    all_to_all x1 -> x0, waiting for transfers between devices: 4.85 us -> none  [body(): lax.all_to_all(down.reshape(shards, share_rows, width), SHARD_AXES, 0, 0)]
  transfers between devices with their start and end apart: 1 -> 0, of which waited for: 1 -> 0; matrix products, arithmetic and copies ran while one was open for 0% -> 0% of each run, Pallas kernels for 0% -> 0%
where the time goes in v3:
time: 105 us
  blocking collectives  97.2 us (93%)
  Pallas kernels  7 us (7%)
    all_to_all x1, blocking collectives, body(): attended = lax.all_to_all(attended, DP_AXES, 0, 0)  19.7 us
    all_to_all x1, blocking collectives, body(): lax.all_to_all(sent.reshape(near, half, sent.shape[2]), NEAR_AXES, 0, 0)  16.2 us
    all_to_all x1, blocking collectives, body(): hidden = lax.all_to_all(finish(came, groups), DP_AXES, 0, 0)  15.3 us
    all_to_all x1, blocking collectives, body(): lax.all_to_all(down.reshape(shards, share_rows, width), SHARD_AXES, 0, 0)  12.9 us
    all_to_all x1, blocking collectives, body(): attended = merge(lax.all_to_all(parts, SHARD_AXES, 0, 0), groups)  11.8 us
    all_to_all x1, blocking collectives, body(): lax.all_to_all(project(attended, out_weight, shards), SHARD_AXES, 0, 0)  11.5 us
    all_to_all x1, blocking collectives, body(): lax.all_to_all(sent.reshape(far, half // far, sent.shape[1]), FAR_AXES, 0...  9.73 us
    pallas_call x1, Pallas kernels, attend(): pl.pallas_call(attend_kernel, out_shape=jax.ShapeDtypeStruct((KVH, ROWS_D...  5.32 us

profile of v3, /device:TPU:1, one launch (start us, length us, event | category | flops | bytes accessed | tf_op | source)
XLA Modules:
  0.0 105.0 jit_solution(4671628467838110779)
XLA Ops:
  0.0 5.3 %attend.1 = f32[8,16,256]{2,1,0:T(8,128)} custom-call(s32[1,1,24]{2,1,0:T(1,128)} %table_hbm.1, s32[2]{0:T(128)} %lengths_hbm.1, bf16[2,8192]{1,0:T(2,128)(2,1)} %q_hbm.1, bf16[2,1024]{1,0:T(2,128)(2,1)} %nk_hbm.1, bf16[2,1024]{1,0:T(2,128)(2,1)} %nv_hbm.1, bf16[1536,1024]{1,0:T(8,128)(2,1)} %bitcast.9, bf16[1536,1024]{1,0:T(8,128)(2,1)} %bitcast.10), custom_call_target="tpu_custom_call" | custom-call | tf_op jit(solution)/shard_map/attend/pallas_call | solution.py:146
  5.3 11.8 %all_to_all.35.parts_ref = f32[8,16,256]{2,1,0:T(8,128)S(1)} all-to-all(f32[8,16,256]{2,1,0:T(8,128)} %attend.1), channel_id=1, replica_groups=mesh['z2'=2,'z1'=2,'z0'=2,'y1'=2,'y0'=2,'ctx'=4,'side'=2] {'ctx','side'}, dimensions={0} | all-to-all | bytes 262144 | tf_op jit(solution)/shard_map/all_to_all | solution.py:360
  17.1 0.0 copy-start.5
  17.1 0.2 merge.1
  17.3 19.7 %all_to_all.36.attended_ref = bf16[32,16,128]{2,1,0:T(8,128)(2,1)S(1)} all-to-all(bf16[32,16,128]{2,1,0:T(8,128)(2,1)S(1)} %merge.1), channel_id=1, replica_groups=mesh['z2'=2,'z1'=2,'z0'=2,'y1'=2,'y0'=2,'ctx'=4,'side'=2] {'z2','z1','z0..., dimensions={0} | all-to-all | bytes 262144 | tf_op jit(solution)/shard_map/all_to_all | solution.py:361
  36.9 0.0 copy-done.5
  37.0 0.0 copy-start
  37.0 0.0 copy-start.4
  37.0 0.2 project.1
  37.2 11.5 %all_to_all.37.came_ref = bf16[8,64,256]{2,1,0:T(8,128)(2,1)S(1)} all-to-all(bf16[8,64,256]{2,1,0:T(8,128)(2,1)S(1)} %project.1), channel_id=1, replica_groups=mesh['z2'=2,'z1'=2,'z0'=2,'y1'=2,'y0'=2,'ctx'=4,'side'=2] {'ctx','side'}, dimensions={0} | all-to-all | bytes 524288 | tf_op jit(solution)/shard_map/all_to_all | solution.py:362
  48.7 0.0 copy-done
  48.7 0.0 copy-done.1
  48.7 0.0 copy-done.3
  48.7 0.0 copy-done.4
  48.7 0.7 widen.1
  49.4 16.2 %all_to_all.38 = bf16[8,32,1920]{2,1,0:T(8,128)(2,1)S(1)} all-to-all(bf16[8,32,1920]{2,1,0:T(8,128)(2,1)S(1)} %bitcast.6), channel_id=1, replica_groups=mesh['z2'=2,'z1'=2,'z0'=2,'y1'=2,'y0'=2,'ctx'=4,'side'=2] {'y1','y0','z0'}, dimensions={0} | all-to-all | bytes 1966080 | tf_op jit(solution)/shard_map/all_to_all | solution.py:367
  65.6 0.1 reduce_sum.21
  65.8 9.7 %all_to_all.39.came_ref = bf16[4,8,1920]{2,1,0:T(8,128)(2,1)S(1)} all-to-all(bf16[4,8,1920]{2,1,0:T(8,128)(2,1)S(1)} %bitcast.11), channel_id=1, replica_groups=mesh['z2'=2,'z1'=2,'z0'=2,'y1'=2,'y0'=2,'ctx'=4,'side'=2] {'z2','z1'}, dimensions={0} | all-to-all | bytes 245760 | tf_op jit(solution)/shard_map/all_to_all | solution.py:369
  75.5 0.2 finish.1
  75.7 15.3 %all_to_all.40.hidden_ref = bf16[32,8,896]{2,1,0:T(8,128)(2,1)S(1)} all-to-all(bf16[32,8,896]{2,1,0:T(8,128)(2,1)S(1)} %finish.1), channel_id=1, replica_groups=mesh['z2'=2,'z1'=2,'z0'=2,'y1'=2,'y0'=2,'ctx'=4,'side'=2] {'z2','z1','z0..., dimensions={0} | all-to-all | bytes 917504 | tf_op jit(solution)/shard_map/all_to_all | solution.py:370
  91.0 0.0 copy-done.2
  91.1 0.4 narrow.1
  91.5 12.9 %all_to_all.41 = f32[8,8,256]{2,1,0:T(8,128)S(1)} all-to-all(f32[8,8,256]{2,1,0:T(8,128)S(1)} %bitcast.7), channel_id=1, replica_groups=mesh['z2'=2,'z1'=2,'z0'=2,'y1'=2,'y0'=2,'ctx'=4,'side'=2] {'ctx','side'}, dimensions={0} | all-to-all | bytes 131072 | tf_op jit(solution)/shard_map/all_to_all | solution.py:372
  104.4 0.6 add_convert_fusion
  (4 shorter events, 0.0 us)
Async XLA Ops:
  17.1 19.8 %copy-start.5 = (bf16[1024,256]{1,0:T(8,128)(2,1)S(1)}, bf16[1024,256]{1,0:T(8,128)(2,1)}, u32[]{:S(2)}) copy-start(bf16[1024,256]{1,0:T(8,128)(2,1)} %weight_ref.1) | copy-start | bytes 1572868
  37.0 11.7 %copy-start = (bf16[256,3584]{1,0:T(8,128)(2,1)S(1)}, bf16[256,3584]{1,0:T(8,128)(2,1)}, u32[]{:S(2)}) copy-start(bf16[256,3584]{1,0:T(8,128)(2,1)} %gate_ref.1) | copy-start | bytes 5505028
  37.0 11.7 %copy-start.1 = (bf16[256,3584]{1,0:T(8,128)(2,1)S(1)}, bf16[256,3584]{1,0:T(8,128)(2,1)}, u32[]{:S(2)}) copy-start(bf16[256,3584]{1,0:T(8,128)(2,1)} %up_ref.1) | copy-start | bytes 5505028
  37.0 11.7 %copy-start.3 = (bf16[64,256]{1,0:T(8,128)(2,1)S(1)}, bf16[64,256]{1,0:T(8,128)(2,1)}, u32[]{:S(2)}) copy-start(bf16[64,256]{1,0:T(8,128)(2,1)} %residual_ref.1) | copy-start | bytes 98308
  37.0 11.7 %copy-start.4 = (f32[256]{0:T(256)S(1)}, f32[256]{0:T(256)}, u32[]{:S(2)}) copy-start(f32[256]{0:T(256)} %param.22) | copy-start | bytes 3076
  65.6 25.4 %copy-start.2 = (bf16[3584,256]{1,0:T(8,128)(2,1)S(1)}, bf16[3584,256]{1,0:T(8,128)(2,1)}, u32[]{:S(2)}) copy-start(bf16[3584,256]{1,0:T(8,128)(2,1)} %down_ref.1) | copy-start | bytes 5505028

commit v4 on v3

--- a/solution.py
+++ b/solution.py
@@ -17,15 +17,18 @@
 ROWS_DEV = 2
 SLOTS = ROWS_DEV * PMAX
 TOKENS = SLOTS * PAGE
-QROWS = ROWS_DEV * KVH * G
-CHUNKS = 4
-CHUNK = TOKENS // CHUNKS
+PAIRS = KVH // 2
+KEY_CHUNKS = 3
+VALUE_CHUNKS = 3
+PAIR_ROWS = 2 * ROWS_DEV * G
 NEG = -1e30
 SHARD_AXES = ("ctx", "side")
 DP_AXES = ("z2", "z1", "z0", "y1", "y0")
 NEAR_AXES = ("y1", "y0", "z0")
 FAR_AXES = ("z2", "z1")
-SPREAD_Y = 4
+GATHER_AXES = ("z2", "z1", "z0", "y1", "y0")
+UNIT_AXES = ("y1", "y0")
+HALF_AXES = ("z0",)
 ATTEND_VMEM = 64 * 1024 * 1024
 
 norm_eps = 1e-05
@@ -33,9 +36,20 @@
 bf16 = jnp.bfloat16
 
 
+def bits_of(index, axes):
+    return {a: index >> (len(axes) - 1 - i) & 1 for i, a in enumerate(axes)}
+
+
+def index_of(bits, axes):
+    index = 0
+    for a in axes:
+        index = index * 2 + bits[a]
+    return index
+
+
 def attend_kernel(
     table_hbm, lengths_hbm, q_hbm, nk_hbm, nv_hbm, key_hbm, value_hbm, out_ref,
-    table, lengths, q_two, nk_ref, nv_ref, q_rows, keys, values, q_wide, scores, owner,
+    table, lengths, q_two, nk_ref, nv_ref, q_rows, keys, values, scores, weights, owner,
     small_sem, key_sem, value_sem,
 ):
     shard = lax.axis_index(SHARD_AXES)
@@ -47,97 +61,121 @@
     ]
     for one in small:
         one.start()
-
-    def copy(src, dst, sem, c):
-        rows = pl.ds(c * CHUNK, CHUNK)
-        return pltpu.make_async_copy(src.at[rows], dst.at[rows], sem.at[c])
-
-    for c in range(CHUNKS):
-        copy(key_hbm, keys, key_sem, c).start()
-    for c in range(CHUNKS):
-        copy(value_hbm, values, value_sem, c).start()
-
+    key_step, value_step = TOKENS // KEY_CHUNKS, TOKENS // VALUE_CHUNKS
+    key_copies = [
+        pltpu.make_async_copy(
+            key_hbm.at[pl.ds(c * key_step, key_step)],
+            keys.at[pl.ds(c * key_step, key_step)],
+            key_sem.at[c],
+        )
+        for c in range(KEY_CHUNKS)
+    ]
+    value_copies = [
+        pltpu.make_async_copy(
+            value_hbm.at[pl.ds(c * value_step, value_step)],
+            values.at[pl.ds(c * value_step, value_step)],
+            value_sem.at[c],
+        )
+        for c in range(VALUE_CHUNKS)
+    ]
+    for copy in key_copies:
+        copy.start()
     for one in small:
         one.wait()
+    for copy in value_copies:
+        copy.start()
 
     for k in range(SLOTS):
         owner[table[0, 0, k]] = k
 
-    def limit_of(slot, row):
+    def limits_of(slot):
         k = owner[slot]
         own = lax.div(k, PMAX)
-        page = lax.rem(k, PMAX)
-        start = (page * 8 + shard) * PAGE
-        count = lengths[row] - start
-        return jnp.where(own == row, count, 0)
+        start = (lax.rem(k, PMAX) * 8 + shard) * PAGE
+        return [jnp.where(own == r, lengths[r] - start, 0) for r in range(ROWS_DEV)]
 
     q_all = q_two[...].astype(f32)
-    for n in range(KVH * G):
+    for h in range(KVH):
         for r in range(ROWS_DEV):
-            at = r * KVH * G + n
-            q_rows[at : at + 1, :] = q_all[r : r + 1, n * HD : (n + 1) * HD]
-    q = q_rows[...].astype(bf16)
-    head_of_row = lax.rem(lax.div(lax.broadcasted_iota(jnp.int32, (QROWS, HD), 0), G), KVH)
-    for h in range(KVH):
-        q_wide[:, h * HD : (h + 1) * HD] = jnp.where(head_of_row == h, q, jnp.zeros_like(q))
-
-    scale = 1.0 / math.sqrt(HD)
-
-    def per_group(ref):
+            for g in range(G):
+                at = (h // 2) * PAIR_ROWS + r * 2 * G + (h % 2) * G + g
+                n = h * G + g
+                q_rows[at : at + 1, :] = q_all[r : r + 1, n * HD : (n + 1) * HD]
+    row = lax.broadcasted_iota(jnp.int32, (PAIR_ROWS, HD), 0)
+    second = lax.rem(lax.div(row, G), 2) == 1
+
+    lane = lax.broadcasted_iota(jnp.int32, (2 * G, HD), 1)
+    within = lax.rem(lane, PAGE)
+    first_half = lane < PAGE
+    bias = []
+    for t in range(TOKENS // HD):
+        left, right = limits_of(2 * t), limits_of(2 * t + 1)
+        halves = [
+            jnp.where(within < jnp.where(first_half, left[r], right[r]), 0.0, NEG)
+            for r in range(ROWS_DEV)
+        ]
+        bias.append(jnp.concatenate(halves, axis=0))
+    bias = jnp.concatenate(bias, axis=1)
+
+    def per_group(ref, j):
         parts = []
         for r in range(ROWS_DEV):
-            for h in range(KVH):
+            for h in (2 * j, 2 * j + 1):
                 one = ref[r : r + 1, h * HD : (h + 1) * HD].astype(f32)
                 parts.append(jnp.broadcast_to(one, (G, HD)))
         return jnp.concatenate(parts, axis=0)
 
-    fresh = jnp.sum(q.astype(f32) * per_group(nk_ref), axis=1, keepdims=True) * scale
-    fresh = jnp.where(shard == 0, fresh, NEG)
-    new_values = per_group(nv_ref)
-
-    lane = lax.broadcasted_iota(jnp.int32, (QROWS // ROWS_DEV, HD), 1)
-    within = lax.rem(lane, PAGE)
-    first_half = lane < PAGE
-    peak = fresh
-    for c in range(CHUNKS):
-        copy(key_hbm, keys, key_sem, c).wait()
-        part = lax.dot_general(
-            q_wide[...], keys[c * CHUNK : (c + 1) * CHUNK, :],
-            (((1,), (1,)), ((), ())), preferred_element_type=f32,
-        ) * scale
-        for t in range(CHUNK // HD):
-            slot = (c * CHUNK + t * HD) // PAGE
-            tiles = []
-            for r in range(ROWS_DEV):
-                live = within < jnp.where(first_half, limit_of(slot, r), limit_of(slot + 1, r))
-                tile = part[r * KVH * G : (r + 1) * KVH * G, t * HD : (t + 1) * HD]
-                tiles.append(jnp.where(live, tile, NEG))
-            tile = jnp.concatenate(tiles, axis=0)
-            scores[:, c * CHUNK + t * HD : c * CHUNK + (t + 1) * HD] = tile
-            peak = jnp.maximum(peak, jnp.max(tile, axis=1, keepdims=True))
-
-    total = jnp.zeros((QROWS, HD), f32)
-    mixed = jnp.zeros((QROWS, KVH * HD), f32)
-    for c in range(CHUNKS):
-        part = scores[:, c * CHUNK : (c + 1) * CHUNK]
-        weight = jnp.where(part > 0.5 * NEG, jnp.exp(part - peak), 0.0)
-        for t in range(CHUNK // HD):
-            total = total + weight[:, t * HD : (t + 1) * HD]
-        copy(value_hbm, values, value_sem, c).wait()
-        mixed = mixed + jnp.dot(
-            weight.astype(bf16), values[c * CHUNK : (c + 1) * CHUNK, :], preferred_element_type=f32
+    scale = 1.0 / math.sqrt(HD)
+    wides = []
+    for j in range(PAIRS):
+        q = q_rows[j * PAIR_ROWS : (j + 1) * PAIR_ROWS, :]
+        wides.append(
+            jnp.concatenate([jnp.where(second, 0.0, q), jnp.where(second, q, 0.0)], axis=1).astype(
+                bf16
+            )
         )
-    fresh_weight = jnp.where(shard == 0, jnp.exp(fresh - peak), 0.0)
-    total = jnp.sum(total, axis=1, keepdims=True) + fresh_weight
-    added = fresh_weight * new_values
-    stat_lane = lax.broadcasted_iota(jnp.int32, (QROWS, HD), 1)
-    stats = jnp.where(stat_lane == 0, peak, total)
-    for h in range(KVH):
+    for c in range(KEY_CHUNKS):
+        key_copies[c].wait()
+        tokens = slice(c * key_step, (c + 1) * key_step)
+        for j in range(PAIRS):
+            scores[j * PAIR_ROWS : (j + 1) * PAIR_ROWS, tokens] = bias[:, tokens] + lax.dot_general(
+                wides[j],
+                keys[tokens, j * 2 * HD : (j + 1) * 2 * HD],
+                (((1,), (1,)), ((), ())),
+                preferred_element_type=f32,
+            )
+    stat_lane = lax.broadcasted_iota(jnp.int32, (PAIR_ROWS, HD), 1)
+    added, stats = [], []
+    for j in range(PAIRS):
+        rows = slice(j * PAIR_ROWS, (j + 1) * PAIR_ROWS)
+        fresh = jnp.sum(q_rows[rows, :] * per_group(nk_ref, j), axis=1, keepdims=True)
+        fresh = jnp.where(shard == 0, fresh, NEG)
+        peak = jnp.maximum(jnp.max(scores[rows, :], axis=1, keepdims=True), fresh)
+        peak = jnp.maximum(peak, 0.1 * NEG)
+        weight = jnp.exp((scores[rows, :] - peak) * scale)
+        fresh_weight = jnp.exp((fresh - peak) * scale)
+        total = jnp.sum(weight, axis=1, keepdims=True) + fresh_weight
+        weights[rows, :] = weight.astype(bf16)
+        stats.append(jnp.where(stat_lane == 0, peak * scale, total))
+        added.append(fresh_weight * per_group(nv_ref, j))
+    mixed = [jnp.zeros((PAIR_ROWS, 2 * HD), f32) for _ in range(PAIRS)]
+    for c in range(VALUE_CHUNKS):
+        value_copies[c].wait()
+        tokens = slice(c * value_step, (c + 1) * value_step)
+        for j in range(PAIRS):
+            mixed[j] = mixed[j] + jnp.dot(
+                weights[j * PAIR_ROWS : (j + 1) * PAIR_ROWS, tokens],
+                values[tokens, j * 2 * HD : (j + 1) * 2 * HD],
+                preferred_element_type=f32,
+            )
+    for j in range(PAIRS):
         for r in range(ROWS_DEV):
-            at = (r * KVH + h) * G
-            own = mixed[at : at + G, h * HD : (h + 1) * HD] + added[at : at + G, :]
-            out_ref[h, r * G : (r + 1) * G, 0:HD] = own
-            out_ref[h, r * G : (r + 1) * G, HD : 2 * HD] = stats[at : at + G, :]
+            for n in range(2):
+                at = (2 * r + n) * G
+                rows = slice(r * G, (r + 1) * G)
+                own = mixed[j][at : at + G, n * HD : (n + 1) * HD] + added[j][at : at + G, :]
+                out_ref[2 * j + n, rows, 0:HD] = own
+                out_ref[2 * j + n, rows, HD : 2 * HD] = stats[j][at : at + G, :]
 
 
 def attend(table, lengths, q, new_key, new_value, keys, values):
@@ -154,15 +192,15 @@
             pltpu.VMEM((ROWS_DEV, KVH * G * HD), bf16),
             pltpu.VMEM((ROWS_DEV, KVH * HD), bf16),
             pltpu.VMEM((ROWS_DEV, KVH * HD), bf16),
-            pltpu.VMEM((QROWS, HD), f32),
+            pltpu.VMEM((PAIRS * PAIR_ROWS, HD), f32),
             pltpu.VMEM((TOKENS, KVH * HD), bf16),
             pltpu.VMEM((TOKENS, KVH * HD), bf16),
-            pltpu.VMEM((QROWS, KVH * HD), bf16),
-            pltpu.VMEM((QROWS, TOKENS), f32),
+            pltpu.VMEM((PAIRS * PAIR_ROWS, TOKENS), f32),
+            pltpu.VMEM((PAIRS * PAIR_ROWS, TOKENS), bf16),
             pltpu.SMEM((SLOTS,), jnp.int32),
             pltpu.SemaphoreType.DMA((5,)),
-            pltpu.SemaphoreType.DMA((CHUNKS,)),
-            pltpu.SemaphoreType.DMA((CHUNKS,)),
+            pltpu.SemaphoreType.DMA((KEY_CHUNKS,)),
+            pltpu.SemaphoreType.DMA((VALUE_CHUNKS,)),
         ],
         compiler_params=pltpu.CompilerParams(vmem_limit_bytes=ATTEND_VMEM),
         name="attend",
@@ -240,24 +278,35 @@
     high = squares.astype(bf16).astype(f32)
     lane = lax.broadcasted_iota(jnp.int32, (middle.shape[0], HD), 1)
     tail = jnp.where(lane == 0, high, jnp.where(lane == 1, squares - high, 0.0)).astype(bf16)
-    blocks = sent_ref.shape[0]
+    blocks = 2 ** len(UNIT_AXES)
+    half = sent_ref.shape[1]
     units = gate_ref.shape[1] // blocks
+    targets = [bits_of(i, NEAR_AXES) for i in range(sent_ref.shape[0])]
     for b in range(blocks):
-        for n, weight_ref in enumerate((gate_ref, up_ref)):
-            sent_ref[b, :, n * units : (n + 1) * units] = jnp.dot(
+        parts = [
+            jnp.dot(
                 scaled, weight_ref[:, b * units : (b + 1) * units], preferred_element_type=f32
             ).astype(bf16)
-        sent_ref[b, :, 2 * units :] = tail
-
-
-def widen(came, residual, gain, gate_weight, up_weight, blocks, share):
+            for weight_ref in (gate_ref, up_ref)
+        ]
+        for i, bits in enumerate(targets):
+            if index_of(bits, UNIT_AXES) != b:
+                continue
+            at = index_of(bits, HALF_AXES) * half
+            for n in range(2):
+                sent_ref[i, :, n * units : (n + 1) * units] = parts[n][at : at + half, :]
+            sent_ref[i, :, 2 * units :] = tail[at : at + half, :]
+
+
+def widen(came, residual, gain, gate_weight, up_weight, share):
     rows, width = residual.shape
-    units = gate_weight.shape[1] // blocks
+    members, halves = 2 ** len(NEAR_AXES), 2 ** len(HALF_AXES)
+    units = gate_weight.shape[1] * halves // members
     vmem = pl.BlockSpec(memory_space=pltpu.VMEM)
     return pl.pallas_call(
         widen_kernel,
         out_shape=(
-            jax.ShapeDtypeStruct((blocks, rows, 2 * units + HD), bf16),
+            jax.ShapeDtypeStruct((members, rows // halves, 2 * units + HD), bf16),
             jax.ShapeDtypeStruct((share, width), f32),
         ),
         in_specs=[vmem] * 5,
@@ -300,9 +349,11 @@
     blocks = down_ref.shape[0] // units
     total = jnp.zeros(out_ref.shape, f32)
     for b in range(blocks):
-        for n in range(groups // blocks):
-            place = (n % 2) * (groups // blocks // 2) + n // 2
-            rows_ref[b, place * rows : (place + 1) * rows, :] = hidden_ref[n * blocks + b].astype(f32)
+        for i in range(groups):
+            bits = bits_of(i, GATHER_AXES)
+            if index_of(bits, UNIT_AXES) == b:
+                at = index_of(bits, HALF_AXES + FAR_AXES) * rows
+                rows_ref[b, at : at + rows, :] = hidden_ref[i].astype(f32)
         total = total + jnp.dot(
             rows_ref[b].astype(bf16),
             down_ref[b * units : (b + 1) * units, :],
@@ -344,7 +395,7 @@
 ):
     shards = lax.axis_size(SHARD_AXES)
     groups = lax.axis_size(DP_AXES)
-    near, far = lax.axis_size(NEAR_AXES), lax.axis_size(FAR_AXES)
+    far = lax.axis_size(FAR_AXES)
     rows, width = residual.shape
     share_rows = rows // shards
 
@@ -361,13 +412,12 @@
     attended = lax.all_to_all(attended, DP_AXES, 0, 0)
     came = lax.all_to_all(project(attended, out_weight, shards), SHARD_AXES, 0, 0)
     sent, middle_own = widen(
-        came, residual, norm_gain.reshape(1, width), gate_weight, up_weight, SPREAD_Y, share_rows
+        came, residual, norm_gain.reshape(1, width), gate_weight, up_weight, share_rows
     )
-    half = rows * SPREAD_Y // near
-    came = lax.all_to_all(sent.reshape(near, half, sent.shape[2]), NEAR_AXES, 0, 0)
+    came = lax.all_to_all(sent, NEAR_AXES, 0, 0)
     sent = jnp.sum(came.astype(f32), axis=0).astype(bf16)
-    came = lax.all_to_all(sent.reshape(far, half // far, sent.shape[1]), FAR_AXES, 0, 0)
-    hidden = lax.all_to_all(finish(came, groups), DP_AXES, 0, 0)
+    came = lax.all_to_all(sent.reshape(far, sent.shape[0] // far, sent.shape[1]), FAR_AXES, 0, 0)
+    hidden = lax.all_to_all(finish(came, groups), GATHER_AXES, 0, 0)
     down = narrow(hidden, down_weight)
     down = lax.all_to_all(down.reshape(shards, share_rows, width), SHARD_AXES, 0, 0)
     return (middle_own + jnp.sum(down, axis=0)).astype(bf16)

time: 105 us -> 104 us (level)
  no operation moved by 1% of the time
where the time goes in v4:
time: 104 us
  blocking collectives  97.2 us (93%)
  Pallas kernels  6.02 us (6%)
    all_to_all x1, blocking collectives, body(): attended = lax.all_to_all(attended, DP_AXES, 0, 0)  19.7 us
    all_to_all x1, blocking collectives, body(): came = lax.all_to_all(sent, NEAR_AXES, 0, 0)  16.2 us
    all_to_all x1, blocking collectives, body(): hidden = lax.all_to_all(finish(came, groups), GATHER_AXES, 0, 0)  15.3 us
    all_to_all x1, blocking collectives, body(): lax.all_to_all(down.reshape(shards, share_rows, width), SHARD_AXES, 0, 0)  12.9 us
    all_to_all x1, blocking collectives, body(): attended = merge(lax.all_to_all(parts, SHARD_AXES, 0, 0), groups)  11.8 us
    all_to_all x1, blocking collectives, body(): lax.all_to_all(project(attended, out_weight, shards), SHARD_AXES, 0, 0)  11.5 us
    all_to_all x1, blocking collectives, body(): lax.all_to_all(sent.reshape(far, sent.shape[0] // far, sent.shape[1]), FA...  9.73 us
    pallas_call x1, Pallas kernels, attend(): pl.pallas_call(attend_kernel, out_shape=jax.ShapeDtypeStruct((KVH, ROWS_D...  4.33 us

profile of v4, /device:TPU:1, one launch (start us, length us, event | category | flops | bytes accessed | tf_op | source)
XLA Modules:
  0.0 104.0 jit_solution(14542285987210791711)
XLA Ops:
  0.0 4.3 %attend.1 = f32[8,16,256]{2,1,0:T(8,128)} custom-call(s32[1,1,24]{2,1,0:T(1,128)} %table_hbm.1, s32[2]{0:T(128)} %lengths_hbm.1, bf16[2,8192]{1,0:T(2,128)(2,1)} %q_hbm.1, bf16[2,1024]{1,0:T(2,128)(2,1)} %nk_hbm.1, bf16[2,1024]{1,0:T(2,128)(2,1)} %nv_hbm.1, bf16[1536,1024]{1,0:T(8,128)(2,1)} %bitcast.7, bf16[1536,1024]{1,0:T(8,128)(2,1)} %bitcast.8), custom_call_target="tpu_custom_call" | custom-call | tf_op jit(solution)/shard_map/attend/pallas_call | solution.py:184
  4.3 11.8 %all_to_all.35.parts_ref = f32[8,16,256]{2,1,0:T(8,128)S(1)} all-to-all(f32[8,16,256]{2,1,0:T(8,128)} %attend.1), channel_id=1, replica_groups=mesh['z2'=2,'z1'=2,'z0'=2,'y1'=2,'y0'=2,'ctx'=4,'side'=2] {'ctx','side'}, dimensions={0} | all-to-all | bytes 262144 | tf_op jit(solution)/shard_map/all_to_all | solution.py:411
  16.1 0.0 copy-start.5
  16.1 0.2 merge.1
  16.3 19.7 %all_to_all.36.attended_ref = bf16[32,16,128]{2,1,0:T(8,128)(2,1)S(1)} all-to-all(bf16[32,16,128]{2,1,0:T(8,128)(2,1)S(1)} %merge.1), channel_id=1, replica_groups=mesh['z2'=2,'z1'=2,'z0'=2,'y1'=2,'y0'=2,'ctx'=4,'side'=2] {'z2','z1','z0..., dimensions={0} | all-to-all | bytes 262144 | tf_op jit(solution)/shard_map/all_to_all | solution.py:412
  36.0 0.0 copy-done.5
  36.0 0.0 copy-start
  36.0 0.0 copy-start.4
  36.0 0.2 project.1
  36.2 11.5 %all_to_all.37.came_ref = bf16[8,64,256]{2,1,0:T(8,128)(2,1)S(1)} all-to-all(bf16[8,64,256]{2,1,0:T(8,128)(2,1)S(1)} %project.1), channel_id=1, replica_groups=mesh['z2'=2,'z1'=2,'z0'=2,'y1'=2,'y0'=2,'ctx'=4,'side'=2] {'ctx','side'}, dimensions={0} | all-to-all | bytes 524288 | tf_op jit(solution)/shard_map/all_to_all | solution.py:413
  47.7 0.0 copy-done
  47.7 0.0 copy-done.1
  47.7 0.0 copy-done.3
  47.7 0.0 copy-done.4
  47.7 0.7 widen.1
  48.4 16.2 %all_to_all.38 = bf16[8,32,1920]{2,1,0:T(8,128)(2,1)S(1)} all-to-all(bf16[8,32,1920]{2,1,0:T(8,128)(2,1)S(1)} %get-tuple-element.8), channel_id=1, replica_groups=mesh['z2'=2,'z1'=2,'z0'=2,'y1'=2,'y0'=2,'ctx'=4,'side'=2] {'y1','y0','z0'}, dimensions={0} | all-to-all | bytes 1966080 | tf_op jit(solution)/shard_map/all_to_all | solution.py:417
  64.7 0.1 reduce_sum.21
  64.8 9.7 %all_to_all.39.came_ref = bf16[4,8,1920]{2,1,0:T(8,128)(2,1)S(1)} all-to-all(bf16[4,8,1920]{2,1,0:T(8,128)(2,1)S(1)} %bitcast.9), channel_id=1, replica_groups=mesh['z2'=2,'z1'=2,'z0'=2,'y1'=2,'y0'=2,'ctx'=4,'side'=2] {'z2','z1'}, dimensions={0} | all-to-all | bytes 245760 | tf_op jit(solution)/shard_map/all_to_all | solution.py:419
  74.5 0.2 finish.1
  74.7 15.3 %all_to_all.40.hidden_ref = bf16[32,8,896]{2,1,0:T(8,128)(2,1)S(1)} all-to-all(bf16[32,8,896]{2,1,0:T(8,128)(2,1)S(1)} %finish.1), channel_id=1, replica_groups=mesh['z2'=2,'z1'=2,'z0'=2,'y1'=2,'y0'=2,'ctx'=4,'side'=2] {'z2','z1','z0..., dimensions={0} | all-to-all | bytes 917504 | tf_op jit(solution)/shard_map/all_to_all | solution.py:420
  90.1 0.0 copy-done.2
  90.1 0.4 narrow.1
  90.5 12.9 %all_to_all.41 = f32[8,8,256]{2,1,0:T(8,128)S(1)} all-to-all(f32[8,8,256]{2,1,0:T(8,128)S(1)} %bitcast.5), channel_id=1, replica_groups=mesh['z2'=2,'z1'=2,'z0'=2,'y1'=2,'y0'=2,'ctx'=4,'side'=2] {'ctx','side'}, dimensions={0} | all-to-all | bytes 131072 | tf_op jit(solution)/shard_map/all_to_all | solution.py:422
  103.4 0.6 add_convert_fusion
  (4 shorter events, 0.0 us)
Async XLA Ops:
  16.1 19.8 %copy-start.5 = (bf16[1024,256]{1,0:T(8,128)(2,1)S(1)}, bf16[1024,256]{1,0:T(8,128)(2,1)}, u32[]{:S(2)}) copy-start(bf16[1024,256]{1,0:T(8,128)(2,1)} %weight_ref.1) | copy-start | bytes 1572868
  36.0 11.7 %copy-start = (bf16[256,3584]{1,0:T(8,128)(2,1)S(1)}, bf16[256,3584]{1,0:T(8,128)(2,1)}, u32[]{:S(2)}) copy-start(bf16[256,3584]{1,0:T(8,128)(2,1)} %gate_ref.1) | copy-start | bytes 5505028
  36.0 11.7 %copy-start.1 = (bf16[256,3584]{1,0:T(8,128)(2,1)S(1)}, bf16[256,3584]{1,0:T(8,128)(2,1)}, u32[]{:S(2)}) copy-start(bf16[256,3584]{1,0:T(8,128)(2,1)} %up_ref.1) | copy-start | bytes 5505028
  36.0 11.7 %copy-start.3 = (bf16[64,256]{1,0:T(8,128)(2,1)S(1)}, bf16[64,256]{1,0:T(8,128)(2,1)}, u32[]{:S(2)}) copy-start(bf16[64,256]{1,0:T(8,128)(2,1)} %residual_ref.1) | copy-start | bytes 98308
  36.0 11.7 %copy-start.4 = (f32[256]{0:T(256)S(1)}, f32[256]{0:T(256)}, u32[]{:S(2)}) copy-start(f32[256]{0:T(256)} %param.22) | copy-start | bytes 3076
  64.7 25.4 %copy-start.2 = (bf16[3584,256]{1,0:T(8,128)(2,1)S(1)}, bf16[3584,256]{1,0:T(8,128)(2,1)}, u32[]{:S(2)}) copy-start(bf16[3584,256]{1,0:T(8,128)(2,1)} %down_ref.1) | copy-start | bytes 5505028

commit v5 on v4

--- a/solution.py
+++ b/solution.py
@@ -156,7 +156,14 @@
         fresh_weight = jnp.exp((fresh - peak) * scale)
         total = jnp.sum(weight, axis=1, keepdims=True) + fresh_weight
         weights[rows, :] = weight.astype(bf16)
-        stats.append(jnp.where(stat_lane == 0, peak * scale, total))
+        own_stats = jnp.zeros((PAIR_ROWS, HD), f32)
+        for n, value in enumerate((peak * scale, total)):
+            rest = value
+            for i in range(3):
+                part = rest.astype(bf16).astype(f32)
+                own_stats = jnp.where(stat_lane == 3 * n + i, part, own_stats)
+                rest = rest - part
+        stats.append(own_stats)
         added.append(fresh_weight * per_group(nv_ref, j))
     mixed = [jnp.zeros((PAIR_ROWS, 2 * HD), f32) for _ in range(PAIRS)]
     for c in range(VALUE_CHUNKS):
@@ -169,13 +176,14 @@
                 preferred_element_type=f32,
             )
     for j in range(PAIRS):
-        for r in range(ROWS_DEV):
-            for n in range(2):
+        for n in range(2):
+            own, own_stats = [], []
+            for r in range(ROWS_DEV):
                 at = (2 * r + n) * G
-                rows = slice(r * G, (r + 1) * G)
-                own = mixed[j][at : at + G, n * HD : (n + 1) * HD] + added[j][at : at + G, :]
-                out_ref[2 * j + n, rows, 0:HD] = own
-                out_ref[2 * j + n, rows, HD : 2 * HD] = stats[j][at : at + G, :]
+                own.append(mixed[j][at : at + G, n * HD : (n + 1) * HD] + added[j][at : at + G, :])
+                own_stats.append(stats[j][at : at + G, :])
+            out_ref[2 * j + n, :, 0:HD] = jnp.concatenate(own, axis=0).astype(bf16)
+            out_ref[2 * j + n, :, HD : 2 * HD] = jnp.concatenate(own_stats, axis=0).astype(bf16)
 
 
 def attend(table, lengths, q, new_key, new_value, keys, values):
@@ -183,7 +191,7 @@
     hbm = pl.BlockSpec(memory_space=pltpu.HBM)
     return pl.pallas_call(
         attend_kernel,
-        out_shape=jax.ShapeDtypeStruct((KVH, ROWS_DEV * G, 2 * HD), f32),
+        out_shape=jax.ShapeDtypeStruct((KVH, ROWS_DEV * G, 2 * HD), bf16),
         in_specs=[hbm] * 7,
         out_specs=vmem,
         scratch_shapes=[
@@ -209,15 +217,20 @@
 
 def merge_kernel(parts_ref, out_ref):
     shards = parts_ref.shape[0]
-    peak = parts_ref[0, :, HD : HD + 1]
+    peaks, totals = [], []
+    for s in range(shards):
+        stats = parts_ref[s, :, HD : 2 * HD].astype(f32)
+        peaks.append(stats[:, 0:1] + stats[:, 1:2] + stats[:, 2:3])
+        totals.append(stats[:, 3:4] + stats[:, 4:5] + stats[:, 5:6])
+    peak = peaks[0]
     for s in range(1, shards):
-        peak = jnp.maximum(peak, parts_ref[s, :, HD : HD + 1])
+        peak = jnp.maximum(peak, peaks[s])
     total = jnp.zeros_like(peak)
     mixed = jnp.zeros((ROWS_DEV * G, HD), f32)
     for s in range(shards):
-        factor = jnp.exp(parts_ref[s, :, HD : HD + 1] - peak)
-        total = total + factor * parts_ref[s, :, HD + 1 : HD + 2]
-        mixed = mixed + factor * parts_ref[s, :, 0:HD]
+        factor = jnp.exp(peaks[s] - peak)
+        total = total + factor * totals[s]
+        mixed = mixed + factor * parts_ref[s, :, 0:HD].astype(f32)
     attended = (mixed / total).astype(bf16)
     for i in range(out_ref.shape[0]):
         out_ref[i] = attended
@@ -359,7 +372,7 @@
             down_ref[b * units : (b + 1) * units, :],
             preferred_element_type=f32,
         )
-    out_ref[...] = total
+    out_ref[...] = total.astype(bf16)
 
 
 def narrow(hidden, down_weight):
@@ -369,7 +382,7 @@
     vmem = pl.BlockSpec(memory_space=pltpu.VMEM)
     return pl.pallas_call(
         narrow_kernel,
-        out_shape=jax.ShapeDtypeStruct((all_rows, down_weight.shape[1]), f32),
+        out_shape=jax.ShapeDtypeStruct((all_rows, down_weight.shape[1]), bf16),
         in_specs=[vmem, vmem],
         out_specs=vmem,
         scratch_shapes=[pltpu.VMEM((blocks, all_rows, units), f32)],
@@ -420,7 +433,7 @@
     hidden = lax.all_to_all(finish(came, groups), GATHER_AXES, 0, 0)
     down = narrow(hidden, down_weight)
     down = lax.all_to_all(down.reshape(shards, share_rows, width), SHARD_AXES, 0, 0)
-    return (middle_own + jnp.sum(down, axis=0)).astype(bf16)
+    return (middle_own + jnp.sum(down.astype(f32), axis=0)).astype(bf16)
 
 
 def solution(mesh):

time: 104 us -> 104 us (level)
  no operation moved by 1% of the time
where the time goes in v5:
time: 104 us
  blocking collectives  96.6 us (93%)
  Pallas kernels  6.08 us (6%)
    all_to_all x1, blocking collectives, body(): attended = lax.all_to_all(attended, DP_AXES, 0, 0)  19.7 us
    all_to_all x1, blocking collectives, body(): came = lax.all_to_all(sent, NEAR_AXES, 0, 0)  16.3 us
    all_to_all x1, blocking collectives, body(): hidden = lax.all_to_all(finish(came, groups), GATHER_AXES, 0, 0)  15.5 us
    all_to_all x1, blocking collectives, body(): lax.all_to_all(down.reshape(shards, share_rows, width), SHARD_AXES, 0, 0)  12.6 us
    all_to_all x1, blocking collectives, body(): lax.all_to_all(project(attended, out_weight, shards), SHARD_AXES, 0, 0)  11.4 us
    all_to_all x1, blocking collectives, body(): attended = merge(lax.all_to_all(parts, SHARD_AXES, 0, 0), groups)  11.3 us
    all_to_all x1, blocking collectives, body(): lax.all_to_all(sent.reshape(far, sent.shape[0] // far, sent.shape[1]), FA...  9.73 us
    pallas_call x1, Pallas kernels, attend(): pl.pallas_call(attend_kernel, out_shape=jax.ShapeDtypeStruct((KVH, ROWS_D...  4.33 us

profile of v5, /device:TPU:1, one launch (start us, length us, event | category | flops | bytes accessed | tf_op | source)
XLA Modules:
  0.0 103.5 jit_solution(7300561298903088546)
XLA Ops:
  0.0 4.3 %attend.1 = bf16[8,16,256]{2,1,0:T(8,128)(2,1)} custom-call(s32[1,1,24]{2,1,0:T(1,128)} %table_hbm.1, s32[2]{0:T(128)} %lengths_hbm.1, bf16[2,8192]{1,0:T(2,128)(2,1)} %q_hbm.1, bf16[2,1024]{1,0:T(2,128)(2,1)} %nk_hbm.1, bf16[2,1024]{1,0:T(2,128)(2,1)} %nv_hbm.1, bf16[1536,1024]{1,0:T(8,128)(2,1)} %bitcast.7, bf16[1536,1024]{1,0:T(8,128)(2,1)} %bitcast.8), custom_call_target="tpu_custom_call" | custom-call | tf_op jit(solution)/shard_map/attend/pallas_call | solution.py:192
  4.3 11.3 %all_to_all.35.parts_ref = bf16[8,16,256]{2,1,0:T(8,128)(2,1)S(1)} all-to-all(bf16[8,16,256]{2,1,0:T(8,128)(2,1)} %attend.1), channel_id=1, replica_groups=mesh['z2'=2,'z1'=2,'z0'=2,'y1'=2,'y0'=2,'ctx'=4,'side'=2] {'ctx','side'}, dimensions={0} | all-to-all | bytes 131072 | tf_op jit(solution)/shard_map/all_to_all | solution.py:424
  15.7 0.0 copy-start.5
  15.7 0.2 merge.1
  15.9 19.7 %all_to_all.36.attended_ref = bf16[32,16,128]{2,1,0:T(8,128)(2,1)S(1)} all-to-all(bf16[32,16,128]{2,1,0:T(8,128)(2,1)S(1)} %merge.1), channel_id=1, replica_groups=mesh['z2'=2,'z1'=2,'z0'=2,'y1'=2,'y0'=2,'ctx'=4,'side'=2] {'z2','z1','z0..., dimensions={0} | all-to-all | bytes 262144 | tf_op jit(solution)/shard_map/all_to_all | solution.py:425
  35.6 0.0 copy-done.5
  35.6 0.0 copy-start
  35.6 0.0 copy-start.4
  35.6 0.2 project.1
  35.9 11.4 %all_to_all.37.came_ref = bf16[8,64,256]{2,1,0:T(8,128)(2,1)S(1)} all-to-all(bf16[8,64,256]{2,1,0:T(8,128)(2,1)S(1)} %project.1), channel_id=1, replica_groups=mesh['z2'=2,'z1'=2,'z0'=2,'y1'=2,'y0'=2,'ctx'=4,'side'=2] {'ctx','side'}, dimensions={0} | all-to-all | bytes 524288 | tf_op jit(solution)/shard_map/all_to_all | solution.py:426
  47.3 0.0 copy-done
  47.3 0.0 copy-done.1
  47.3 0.0 copy-done.3
  47.3 0.0 copy-done.4
  47.3 0.7 widen.1
  48.0 16.3 %all_to_all.38 = bf16[8,32,1920]{2,1,0:T(8,128)(2,1)S(1)} all-to-all(bf16[8,32,1920]{2,1,0:T(8,128)(2,1)S(1)} %get-tuple-element.8), channel_id=1, replica_groups=mesh['z2'=2,'z1'=2,'z0'=2,'y1'=2,'y0'=2,'ctx'=4,'side'=2] {'y1','y0','z0'}, dimensions={0} | all-to-all | bytes 1966080 | tf_op jit(solution)/shard_map/all_to_all | solution.py:430
  64.3 0.1 reduce_sum.21
  64.4 9.7 %all_to_all.39.came_ref = bf16[4,8,1920]{2,1,0:T(8,128)(2,1)S(1)} all-to-all(bf16[4,8,1920]{2,1,0:T(8,128)(2,1)S(1)} %bitcast.9), channel_id=1, replica_groups=mesh['z2'=2,'z1'=2,'z0'=2,'y1'=2,'y0'=2,'ctx'=4,'side'=2] {'z2','z1'}, dimensions={0} | all-to-all | bytes 245760 | tf_op jit(solution)/shard_map/all_to_all | solution.py:432
  74.1 0.2 finish.1
  74.4 15.5 %all_to_all.40.hidden_ref = bf16[32,8,896]{2,1,0:T(8,128)(2,1)S(1)} all-to-all(bf16[32,8,896]{2,1,0:T(8,128)(2,1)S(1)} %finish.1), channel_id=1, replica_groups=mesh['z2'=2,'z1'=2,'z0'=2,'y1'=2,'y0'=2,'ctx'=4,'side'=2] {'z2','z1','z0..., dimensions={0} | all-to-all | bytes 917504 | tf_op jit(solution)/shard_map/all_to_all | solution.py:433
  89.9 0.0 copy-done.2
  89.9 0.4 narrow.1
  90.3 12.6 %all_to_all.41 = bf16[8,8,256]{2,1,0:T(8,128)(2,1)S(1)} all-to-all(bf16[8,8,256]{2,1,0:T(8,128)(2,1)S(1)} %bitcast.5), channel_id=1, replica_groups=mesh['z2'=2,'z1'=2,'z0'=2,'y1'=2,'y0'=2,'ctx'=4,'side'=2] {'ctx','side'}, dimensions={0} | all-to-all | bytes 65536 | tf_op jit(solution)/shard_map/all_to_all | solution.py:435
  102.9 0.6 add_convert_fusion
  (4 shorter events, 0.0 us)
Async XLA Ops:
  15.7 19.9 %copy-start.5 = (bf16[1024,256]{1,0:T(8,128)(2,1)S(1)}, bf16[1024,256]{1,0:T(8,128)(2,1)}, u32[]{:S(2)}) copy-start(bf16[1024,256]{1,0:T(8,128)(2,1)} %weight_ref.1) | copy-start | bytes 1572868
  35.6 11.6 %copy-start = (bf16[256,3584]{1,0:T(8,128)(2,1)S(1)}, bf16[256,3584]{1,0:T(8,128)(2,1)}, u32[]{:S(2)}) copy-start(bf16[256,3584]{1,0:T(8,128)(2,1)} %gate_ref.1) | copy-start | bytes 5505028
  35.6 11.6 %copy-start.1 = (bf16[256,3584]{1,0:T(8,128)(2,1)S(1)}, bf16[256,3584]{1,0:T(8,128)(2,1)}, u32[]{:S(2)}) copy-start(bf16[256,3584]{1,0:T(8,128)(2,1)} %up_ref.1) | copy-start | bytes 5505028
  35.6 11.6 %copy-start.3 = (bf16[64,256]{1,0:T(8,128)(2,1)S(1)}, bf16[64,256]{1,0:T(8,128)(2,1)}, u32[]{:S(2)}) copy-start(bf16[64,256]{1,0:T(8,128)(2,1)} %residual_ref.1) | copy-start | bytes 98308
  35.6 11.6 %copy-start.4 = (f32[256]{0:T(256)S(1)}, f32[256]{0:T(256)}, u32[]{:S(2)}) copy-start(f32[256]{0:T(256)} %param.22) | copy-start | bytes 3076
  64.3 25.6 %copy-start.2 = (bf16[3584,256]{1,0:T(8,128)(2,1)S(1)}, bf16[3584,256]{1,0:T(8,128)(2,1)}, u32[]{:S(2)}) copy-start(bf16[3584,256]{1,0:T(8,128)(2,1)} %down_ref.1) | copy-start | bytes 5505028

commit v6 on v5

--- a/solution.py
+++ b/solution.py
@@ -1,3 +1,4 @@
+import itertools
 import math
 
 import jax
@@ -23,11 +24,13 @@
 PAIR_ROWS = 2 * ROWS_DEV * G
 NEG = -1e30
 SHARD_AXES = ("ctx", "side")
+SHARD_SIZES = (4, 2)
 DP_AXES = ("z2", "z1", "z0", "y1", "y0")
 NEAR_AXES = ("y1", "y0", "z0")
 FAR_AXES = ("z2", "z1")
 GATHER_AXES = ("z2", "z1", "z0", "y1", "y0")
 UNIT_AXES = ("y1", "y0")
+Z_AXES = ("z2", "z1", "z0")
 HALF_AXES = ("z0",)
 ATTEND_VMEM = 64 * 1024 * 1024
 
@@ -38,6 +41,14 @@
 
 def bits_of(index, axes):
     return {a: index >> (len(axes) - 1 - i) & 1 for i, a in enumerate(axes)}
+
+
+def gather_members():
+    members = []
+    for i in range(2 ** len(GATHER_AXES)):
+        z, y = i % 8, (i + i // 8) % 4
+        members.append({**bits_of(z, Z_AXES), **bits_of(y, UNIT_AXES)})
+    return members
 
 
 def index_of(bits, axes):
@@ -45,6 +56,28 @@
     for a in axes:
         index = index * 2 + bits[a]
     return index
+
+
+def in_order(members, axes):
+    names = DP_AXES + SHARD_AXES
+    sizes = (2,) * len(DP_AXES) + SHARD_SIZES
+    rest = [i for i, a in enumerate(names) if a not in axes]
+    order = []
+    for fixed in itertools.product(*(range(sizes[i]) for i in rest)):
+        group = []
+        for bits in members:
+            device = 0
+            for i, a in enumerate(names):
+                device = device * sizes[i] + (bits[a] if a in bits else fixed[rest.index(i)])
+            group.append(device)
+        order.append(group)
+    return order
+
+
+def swap(x, members, axes):
+    return lax.all_to_all(
+        x, DP_AXES + SHARD_AXES, 0, 0, axis_index_groups=in_order(members, axes)
+    )
 
 
 def attend_kernel(
@@ -363,7 +396,7 @@
     total = jnp.zeros(out_ref.shape, f32)
     for b in range(blocks):
         for i in range(groups):
-            bits = bits_of(i, GATHER_AXES)
+            bits = gather_members()[i]
             if index_of(bits, UNIT_AXES) == b:
                 at = index_of(bits, HALF_AXES + FAR_AXES) * rows
                 rows_ref[b, at : at + rows, :] = hidden_ref[i].astype(f32)
@@ -430,7 +463,7 @@
     came = lax.all_to_all(sent, NEAR_AXES, 0, 0)
     sent = jnp.sum(came.astype(f32), axis=0).astype(bf16)
     came = lax.all_to_all(sent.reshape(far, sent.shape[0] // far, sent.shape[1]), FAR_AXES, 0, 0)
-    hidden = lax.all_to_all(finish(came, groups), GATHER_AXES, 0, 0)
+    hidden = swap(finish(came, groups), gather_members(), GATHER_AXES)
     down = narrow(hidden, down_weight)
     down = lax.all_to_all(down.reshape(shards, share_rows, width), SHARD_AXES, 0, 0)
     return (middle_own + jnp.sum(down.astype(f32), axis=0)).astype(bf16)

time: 104 us -> 103 us (level)
  blocking collectives: 96.6 us -> 95.4 us
where the time goes in v6:
time: 103 us; the launch traced here: 102 us
  blocking collectives  95.4 us (93%)
  Pallas kernels  6.07 us (6%)
    all_to_all x1, blocking collectives, body(): attended = lax.all_to_all(attended, DP_AXES, 0, 0)  19.7 us
    all_to_all x1, blocking collectives, body(): came = lax.all_to_all(sent, NEAR_AXES, 0, 0)  16.3 us
    all_to_all x1, blocking collectives, swap(): lax.all_to_all(x, DP_AXES + SHARD_AXES, 0, 0, axis_index_groups=in_order(...  15.1 us
    all_to_all x1, blocking collectives, body(): lax.all_to_all(down.reshape(shards, share_rows, width), SHARD_AXES, 0, 0)  11.9 us
    all_to_all x1, blocking collectives, body(): lax.all_to_all(project(attended, out_weight, shards), SHARD_AXES, 0, 0)  11.4 us
    all_to_all x1, blocking collectives, body(): attended = merge(lax.all_to_all(parts, SHARD_AXES, 0, 0), groups)  11.3 us
    all_to_all x1, blocking collectives, body(): lax.all_to_all(sent.reshape(far, sent.shape[0] // far, sent.shape[1]), FA...  9.73 us
    pallas_call x1, Pallas kernels, attend(): pl.pallas_call(attend_kernel, out_shape=jax.ShapeDtypeStruct((KVH, ROWS_D...  4.33 us

profile of v6, /device:TPU:1, one launch (start us, length us, event | category | flops | bytes accessed | tf_op | source)
XLA Modules:
  0.0 102.3 jit_solution(4147395652570072705)
XLA Ops:
  0.0 4.3 %attend.1 = bf16[8,16,256]{2,1,0:T(8,128)(2,1)} custom-call(s32[1,1,24]{2,1,0:T(1,128)} %table_hbm.1, s32[2]{0:T(128)} %lengths_hbm.1, bf16[2,8192]{1,0:T(2,128)(2,1)} %q_hbm.1, bf16[2,1024]{1,0:T(2,128)(2,1)} %nk_hbm.1, bf16[2,1024]{1,0:T(2,128)(2,1)} %nv_hbm.1, bf16[1536,1024]{1,0:T(8,128)(2,1)} %bitcast.7, bf16[1536,1024]{1,0:T(8,128)(2,1)} %bitcast.8), custom_call_target="tpu_custom_call" | custom-call | tf_op jit(solution)/shard_map/attend/pallas_call | solution.py:225
  4.3 11.3 %all_to_all.35.parts_ref = bf16[8,16,256]{2,1,0:T(8,128)(2,1)S(1)} all-to-all(bf16[8,16,256]{2,1,0:T(8,128)(2,1)} %attend.1), channel_id=1, replica_groups=mesh['z2'=2,'z1'=2,'z0'=2,'y1'=2,'y0'=2,'ctx'=4,'side'=2] {'ctx','side'}, dimensions={0} | all-to-all | bytes 131072 | tf_op jit(solution)/shard_map/all_to_all | solution.py:457
  15.7 0.0 copy-start.5
  15.7 0.2 merge.1
  15.9 19.7 %all_to_all.36.attended_ref = bf16[32,16,128]{2,1,0:T(8,128)(2,1)S(1)} all-to-all(bf16[32,16,128]{2,1,0:T(8,128)(2,1)S(1)} %merge.1), channel_id=1, replica_groups=mesh['z2'=2,'z1'=2,'z0'=2,'y1'=2,'y0'=2,'ctx'=4,'side'=2] {'z2','z1','z0..., dimensions={0} | all-to-all | bytes 262144 | tf_op jit(solution)/shard_map/all_to_all | solution.py:458
  35.6 0.0 copy-done.5
  35.6 0.0 copy-start
  35.6 0.0 copy-start.4
  35.6 0.2 project.1
  35.9 11.4 %all_to_all.37.came_ref = bf16[8,64,256]{2,1,0:T(8,128)(2,1)S(1)} all-to-all(bf16[8,64,256]{2,1,0:T(8,128)(2,1)S(1)} %project.1), channel_id=1, replica_groups=mesh['z2'=2,'z1'=2,'z0'=2,'y1'=2,'y0'=2,'ctx'=4,'side'=2] {'ctx','side'}, dimensions={0} | all-to-all | bytes 524288 | tf_op jit(solution)/shard_map/all_to_all | solution.py:459
  47.3 0.0 copy-done
  47.3 0.0 copy-done.1
  47.3 0.0 copy-done.3
  47.3 0.0 copy-done.4
  47.3 0.7 widen.1
  48.0 16.3 %all_to_all.38 = bf16[8,32,1920]{2,1,0:T(8,128)(2,1)S(1)} all-to-all(bf16[8,32,1920]{2,1,0:T(8,128)(2,1)S(1)} %get-tuple-element.8), channel_id=1, replica_groups=mesh['z2'=2,'z1'=2,'z0'=2,'y1'=2,'y0'=2,'ctx'=4,'side'=2] {'y1','y0','z0'}, dimensions={0} | all-to-all | bytes 1966080 | tf_op jit(solution)/shard_map/all_to_all | solution.py:463
  64.3 0.1 reduce_sum.21
  64.4 9.7 %all_to_all.39.came_ref = bf16[4,8,1920]{2,1,0:T(8,128)(2,1)S(1)} all-to-all(bf16[4,8,1920]{2,1,0:T(8,128)(2,1)S(1)} %bitcast.9), channel_id=1, replica_groups=mesh['z2'=2,'z1'=2,'z0'=2,'y1'=2,'y0'=2,'ctx'=4,'side'=2] {'z2','z1'}, dimensions={0} | all-to-all | bytes 245760 | tf_op jit(solution)/shard_map/all_to_all | solution.py:465
  74.1 0.2 finish.1
  74.4 15.1 %all_to_all.40.hidden_ref = bf16[32,8,896]{2,1,0:T(8,128)(2,1)S(1)} all-to-all(bf16[32,8,896]{2,1,0:T(8,128)(2,1)S(1)} %finish.1), channel_id=1, replica_groups={{0,40,80,120,128,168,208,248,8,48,88,96,136,176,216,224,16,56,64,104,14..., dimensions={0} | all-to-all | bytes 917504 | tf_op jit(solution)/shard_map/all_to_all | solution.py:78
  89.5 0.0 copy-done.2
  89.5 0.4 narrow.1
  89.9 11.9 %all_to_all.41 = bf16[8,8,256]{2,1,0:T(8,128)(2,1)S(1)} all-to-all(bf16[8,8,256]{2,1,0:T(8,128)(2,1)S(1)} %bitcast.5), channel_id=1, replica_groups=mesh['z2'=2,'z1'=2,'z0'=2,'y1'=2,'y0'=2,'ctx'=4,'side'=2] {'ctx','side'}, dimensions={0} | all-to-all | bytes 65536 | tf_op jit(solution)/shard_map/all_to_all | solution.py:468
  101.7 0.6 add_convert_fusion
  (4 shorter events, 0.0 us)
Async XLA Ops:
  15.7 19.9 %copy-start.5 = (bf16[1024,256]{1,0:T(8,128)(2,1)S(1)}, bf16[1024,256]{1,0:T(8,128)(2,1)}, u32[]{:S(2)}) copy-start(bf16[1024,256]{1,0:T(8,128)(2,1)} %weight_ref.1) | copy-start | bytes 1572868
  35.6 11.6 %copy-start = (bf16[256,3584]{1,0:T(8,128)(2,1)S(1)}, bf16[256,3584]{1,0:T(8,128)(2,1)}, u32[]{:S(2)}) copy-start(bf16[256,3584]{1,0:T(8,128)(2,1)} %gate_ref.1) | copy-start | bytes 5505028
  35.6 11.6 %copy-start.1 = (bf16[256,3584]{1,0:T(8,128)(2,1)S(1)}, bf16[256,3584]{1,0:T(8,128)(2,1)}, u32[]{:S(2)}) copy-start(bf16[256,3584]{1,0:T(8,128)(2,1)} %up_ref.1) | copy-start | bytes 5505028
  35.6 11.6 %copy-start.3 = (bf16[64,256]{1,0:T(8,128)(2,1)S(1)}, bf16[64,256]{1,0:T(8,128)(2,1)}, u32[]{:S(2)}) copy-start(bf16[64,256]{1,0:T(8,128)(2,1)} %residual_ref.1) | copy-start | bytes 98308
  35.6 11.6 %copy-start.4 = (f32[256]{0:T(256)S(1)}, f32[256]{0:T(256)}, u32[]{:S(2)}) copy-start(f32[256]{0:T(256)} %param.22) | copy-start | bytes 3076
  64.3 25.2 %copy-start.2 = (bf16[3584,256]{1,0:T(8,128)(2,1)S(1)}, bf16[3584,256]{1,0:T(8,128)(2,1)}, u32[]{:S(2)}) copy-start(bf16[3584,256]{1,0:T(8,128)(2,1)} %down_ref.1) | copy-start | bytes 5505028

commit v7 on v6

--- a/solution.py
+++ b/solution.py
@@ -48,6 +48,13 @@
     for i in range(2 ** len(GATHER_AXES)):
         z, y = i % 8, (i + i // 8) % 4
         members.append({**bits_of(z, Z_AXES), **bits_of(y, UNIT_AXES)})
+    return members
+
+
+def near_members():
+    members = []
+    for i in range(2 ** len(NEAR_AXES)):
+        members.append({**bits_of((i + i // 4) % 2, HALF_AXES), **bits_of(i % 4, UNIT_AXES)})
     return members
 
 
@@ -285,7 +292,8 @@
 def project_kernel(attended_ref, weight_ref, out_ref, rows_ref):
     groups = attended_ref.shape[0]
     for n in range(groups):
-        rows_ref[n * ROWS_DEV * G : (n + 1) * ROWS_DEV * G, :] = attended_ref[n].astype(f32)
+        at = index_of(gather_members()[n], DP_AXES) * ROWS_DEV * G
+        rows_ref[at : at + ROWS_DEV * G, :] = attended_ref[n].astype(f32)
     heads = [rows_ref[pl.ds(g, groups * ROWS_DEV, stride=G), :] for g in range(G)]
     wide = jnp.concatenate(heads, axis=1).astype(bf16)
     result = jnp.dot(wide, weight_ref[...], preferred_element_type=f32).astype(bf16)
@@ -327,7 +335,7 @@
     blocks = 2 ** len(UNIT_AXES)
     half = sent_ref.shape[1]
     units = gate_ref.shape[1] // blocks
-    targets = [bits_of(i, NEAR_AXES) for i in range(sent_ref.shape[0])]
+    targets = near_members()
     for b in range(blocks):
         parts = [
             jnp.dot(
@@ -455,12 +463,12 @@
         value_pool.reshape(TOKENS, KVH * HD),
     )
     attended = merge(lax.all_to_all(parts, SHARD_AXES, 0, 0), groups)
-    attended = lax.all_to_all(attended, DP_AXES, 0, 0)
+    attended = swap(attended, gather_members(), DP_AXES)
     came = lax.all_to_all(project(attended, out_weight, shards), SHARD_AXES, 0, 0)
     sent, middle_own = widen(
         came, residual, norm_gain.reshape(1, width), gate_weight, up_weight, share_rows
     )
-    came = lax.all_to_all(sent, NEAR_AXES, 0, 0)
+    came = swap(sent, near_members(), NEAR_AXES)
     sent = jnp.sum(came.astype(f32), axis=0).astype(bf16)
     came = lax.all_to_all(sent.reshape(far, sent.shape[0] // far, sent.shape[1]), FAR_AXES, 0, 0)
     hidden = swap(finish(came, groups), gather_members(), GATHER_AXES)

time: 103 us -> 103 us (level)
    all_to_all x2 -> x0, blocking collectives: 36 us -> none  [the longest x1 19.7 us: body(): attended = lax.all_to_all(attended, DP_AXES, 0, 0)]
    all_to_all x1 -> x3, blocking collectives: 15.1 us -> 50.8 us  [swap(): lax.all_to_all(x, DP_AXES + SHARD_AXES, 0, 0, axis_index_groups=in_order(...]
where the time goes in v7:
time: 103 us; the launch traced here: 102 us
  blocking collectives  95.3 us (93%)
  Pallas kernels  6.07 us (6%)
    all_to_all x3, blocking collectives, swap(): lax.all_to_all(x, DP_AXES + SHARD_AXES, 0, 0, axis_index_groups=in_order(...  50.8 us
    all_to_all x1, blocking collectives, body(): lax.all_to_all(down.reshape(shards, share_rows, width), SHARD_AXES, 0, 0)  12 us
    all_to_all x1, blocking collectives, body(): attended = merge(lax.all_to_all(parts, SHARD_AXES, 0, 0), groups)  11.3 us
    all_to_all x1, blocking collectives, body(): lax.all_to_all(project(attended, out_weight, shards), SHARD_AXES, 0, 0)  11.3 us
    all_to_all x1, blocking collectives, body(): lax.all_to_all(sent.reshape(far, sent.shape[0] // far, sent.shape[1]), FA...  9.77 us
    pallas_call x1, Pallas kernels, attend(): pl.pallas_call(attend_kernel, out_shape=jax.ShapeDtypeStruct((KVH, ROWS_D...  4.33 us

profile of v7, /device:TPU:1, one launch (start us, length us, event | category | flops | bytes accessed | tf_op | source)
XLA Modules:
  0.0 102.2 jit_solution(14772987643196641164)
XLA Ops:
  0.0 4.3 %attend.1 = bf16[8,16,256]{2,1,0:T(8,128)(2,1)} custom-call(s32[1,1,24]{2,1,0:T(1,128)} %table_hbm.1, s32[2]{0:T(128)} %lengths_hbm.1, bf16[2,8192]{1,0:T(2,128)(2,1)} %q_hbm.1, bf16[2,1024]{1,0:T(2,128)(2,1)} %nk_hbm.1, bf16[2,1024]{1,0:T(2,128)(2,1)} %nv_hbm.1, bf16[1536,1024]{1,0:T(8,128)(2,1)} %bitcast.7, bf16[1536,1024]{1,0:T(8,128)(2,1)} %bitcast.8), custom_call_target="tpu_custom_call" | custom-call | tf_op jit(solution)/shard_map/attend/pallas_call | solution.py:232
  4.3 11.3 %all_to_all.35.parts_ref = bf16[8,16,256]{2,1,0:T(8,128)(2,1)S(1)} all-to-all(bf16[8,16,256]{2,1,0:T(8,128)(2,1)} %attend.1), channel_id=1, replica_groups=mesh['z2'=2,'z1'=2,'z0'=2,'y1'=2,'y0'=2,'ctx'=4,'side'=2] {'ctx','side'}, dimensions={0} | all-to-all | bytes 131072 | tf_op jit(solution)/shard_map/all_to_all | solution.py:465
  15.7 0.0 copy-start.5
  15.7 0.2 merge.1
  15.9 19.5 %all_to_all.36.attended_ref = bf16[32,16,128]{2,1,0:T(8,128)(2,1)S(1)} all-to-all(bf16[32,16,128]{2,1,0:T(8,128)(2,1)S(1)} %merge.1), channel_id=1, replica_groups={{0,40,80,120,128,168,208,248,8,48,88,96,136,176,216,224,16,56,64,104,14..., dimensions={0} | all-to-all | bytes 262144 | tf_op jit(solution)/shard_map/all_to_all | solution.py:85
  35.5 0.0 copy-done.5
  35.5 0.0 copy-start
  35.5 0.0 copy-start.4
  35.5 0.2 project.1
  35.7 11.3 %all_to_all.37.came_ref = bf16[8,64,256]{2,1,0:T(8,128)(2,1)S(1)} all-to-all(bf16[8,64,256]{2,1,0:T(8,128)(2,1)S(1)} %project.1), channel_id=1, replica_groups=mesh['z2'=2,'z1'=2,'z0'=2,'y1'=2,'y0'=2,'ctx'=4,'side'=2] {'ctx','side'}, dimensions={0} | all-to-all | bytes 524288 | tf_op jit(solution)/shard_map/all_to_all | solution.py:467
  47.0 0.0 copy-done
  47.0 0.0 copy-done.1
  47.0 0.0 copy-done.3
  47.0 0.0 copy-done.4
  47.0 0.7 widen.1
  47.7 15.9 %all_to_all.38 = bf16[8,32,1920]{2,1,0:T(8,128)(2,1)S(1)} all-to-all(bf16[8,32,1920]{2,1,0:T(8,128)(2,1)S(1)} %get-tuple-element.8), channel_id=1, replica_groups={{0,40,16,56,32,8,48,24},{1,41,17,57,33,9,49,25},{2,42,18,58,34,10,50,26..., dimensions={0} | all-to-all | bytes 1966080 | tf_op jit(solution)/shard_map/all_to_all | solution.py:85
  63.6 0.1 reduce_sum.21
  63.7 9.8 %all_to_all.39.came_ref = bf16[4,8,1920]{2,1,0:T(8,128)(2,1)S(1)} all-to-all(bf16[4,8,1920]{2,1,0:T(8,128)(2,1)S(1)} %bitcast.9), channel_id=1, replica_groups=mesh['z2'=2,'z1'=2,'z0'=2,'y1'=2,'y0'=2,'ctx'=4,'side'=2] {'z2','z1'}, dimensions={0} | all-to-all | bytes 245760 | tf_op jit(solution)/shard_map/all_to_all | solution.py:473
  73.5 0.2 finish.1
  73.7 15.4 %all_to_all.40.hidden_ref = bf16[32,8,896]{2,1,0:T(8,128)(2,1)S(1)} all-to-all(bf16[32,8,896]{2,1,0:T(8,128)(2,1)S(1)} %finish.1), channel_id=1, replica_groups={{0,40,80,120,128,168,208,248,8,48,88,96,136,176,216,224,16,56,64,104,14..., dimensions={0} | all-to-all | bytes 917504 | tf_op jit(solution)/shard_map/all_to_all | solution.py:85
  89.1 0.0 copy-done.2
  89.2 0.4 narrow.1
  89.6 12.0 %all_to_all.41 = bf16[8,8,256]{2,1,0:T(8,128)(2,1)S(1)} all-to-all(bf16[8,8,256]{2,1,0:T(8,128)(2,1)S(1)} %bitcast.5), channel_id=1, replica_groups=mesh['z2'=2,'z1'=2,'z0'=2,'y1'=2,'y0'=2,'ctx'=4,'side'=2] {'ctx','side'}, dimensions={0} | all-to-all | bytes 65536 | tf_op jit(solution)/shard_map/all_to_all | solution.py:476
  101.6 0.6 add_convert_fusion
  (4 shorter events, 0.0 us)
Async XLA Ops:
  15.7 19.8 %copy-start.5 = (bf16[1024,256]{1,0:T(8,128)(2,1)S(1)}, bf16[1024,256]{1,0:T(8,128)(2,1)}, u32[]{:S(2)}) copy-start(bf16[1024,256]{1,0:T(8,128)(2,1)} %weight_ref.1) | copy-start | bytes 1572868
  35.5 11.5 %copy-start = (bf16[256,3584]{1,0:T(8,128)(2,1)S(1)}, bf16[256,3584]{1,0:T(8,128)(2,1)}, u32[]{:S(2)}) copy-start(bf16[256,3584]{1,0:T(8,128)(2,1)} %gate_ref.1) | copy-start | bytes 5505028
  35.5 11.5 %copy-start.1 = (bf16[256,3584]{1,0:T(8,128)(2,1)S(1)}, bf16[256,3584]{1,0:T(8,128)(2,1)}, u32[]{:S(2)}) copy-start(bf16[256,3584]{1,0:T(8,128)(2,1)} %up_ref.1) | copy-start | bytes 5505028
  35.5 11.5 %copy-start.3 = (bf16[64,256]{1,0:T(8,128)(2,1)S(1)}, bf16[64,256]{1,0:T(8,128)(2,1)}, u32[]{:S(2)}) copy-start(bf16[64,256]{1,0:T(8,128)(2,1)} %residual_ref.1) | copy-start | bytes 98308
  35.5 11.5 %copy-start.4 = (f32[256]{0:T(256)S(1)}, f32[256]{0:T(256)}, u32[]{:S(2)}) copy-start(f32[256]{0:T(256)} %param.22) | copy-start | bytes 3076
  63.6 25.5 %copy-start.2 = (bf16[3584,256]{1,0:T(8,128)(2,1)S(1)}, bf16[3584,256]{1,0:T(8,128)(2,1)}, u32[]{:S(2)}) copy-start(bf16[3584,256]{1,0:T(8,128)(2,1)} %down_ref.1) | copy-start | bytes 5505028

commit v8 on v6

--- a/solution.py
+++ b/solution.py
@@ -46,7 +46,7 @@
 def gather_members():
     members = []
     for i in range(2 ** len(GATHER_AXES)):
-        z, y = i % 8, (i + i // 8) % 4
+        z, y = -i % 8, -(i + i // 8) % 4
         members.append({**bits_of(z, Z_AXES), **bits_of(y, UNIT_AXES)})
     return members
 

time: 103 us -> 103 us (level)
  no operation moved by 1% of the time
where the time goes in v8:
time: 103 us; the launch traced here: 102 us
  blocking collectives  95.4 us (93%)
  Pallas kernels  6.07 us (6%)
    all_to_all x1, blocking collectives, body(): attended = lax.all_to_all(attended, DP_AXES, 0, 0)  19.7 us
    all_to_all x1, blocking collectives, body(): came = lax.all_to_all(sent, NEAR_AXES, 0, 0)  16.3 us
    all_to_all x1, blocking collectives, swap(): lax.all_to_all(x, DP_AXES + SHARD_AXES, 0, 0, axis_index_groups=in_order(...  14.1 us
    all_to_all x1, blocking collectives, body(): lax.all_to_all(down.reshape(shards, share_rows, width), SHARD_AXES, 0, 0)  12.8 us
    all_to_all x1, blocking collectives, body(): lax.all_to_all(project(attended, out_weight, shards), SHARD_AXES, 0, 0)  11.4 us
    all_to_all x1, blocking collectives, body(): attended = merge(lax.all_to_all(parts, SHARD_AXES, 0, 0), groups)  11.3 us
    all_to_all x1, blocking collectives, body(): lax.all_to_all(sent.reshape(far, sent.shape[0] // far, sent.shape[1]), FA...  9.73 us
    pallas_call x1, Pallas kernels, attend(): pl.pallas_call(attend_kernel, out_shape=jax.ShapeDtypeStruct((KVH, ROWS_D...  4.33 us

profile of v8, /device:TPU:1, one launch (start us, length us, event | category | flops | bytes accessed | tf_op | source)
XLA Modules:
  0.0 102.3 jit_solution(14652851991560018368)
XLA Ops:
  0.0 4.3 %attend.1 = bf16[8,16,256]{2,1,0:T(8,128)(2,1)} custom-call(s32[1,1,24]{2,1,0:T(1,128)} %table_hbm.1, s32[2]{0:T(128)} %lengths_hbm.1, bf16[2,8192]{1,0:T(2,128)(2,1)} %q_hbm.1, bf16[2,1024]{1,0:T(2,128)(2,1)} %nk_hbm.1, bf16[2,1024]{1,0:T(2,128)(2,1)} %nv_hbm.1, bf16[1536,1024]{1,0:T(8,128)(2,1)} %bitcast.7, bf16[1536,1024]{1,0:T(8,128)(2,1)} %bitcast.8), custom_call_target="tpu_custom_call" | custom-call | tf_op jit(solution)/shard_map/attend/pallas_call | solution.py:225
  4.3 11.3 %all_to_all.35.parts_ref = bf16[8,16,256]{2,1,0:T(8,128)(2,1)S(1)} all-to-all(bf16[8,16,256]{2,1,0:T(8,128)(2,1)} %attend.1), channel_id=1, replica_groups=mesh['z2'=2,'z1'=2,'z0'=2,'y1'=2,'y0'=2,'ctx'=4,'side'=2] {'ctx','side'}, dimensions={0} | all-to-all | bytes 131072 | tf_op jit(solution)/shard_map/all_to_all | solution.py:457
  15.7 0.0 copy-start.5
  15.7 0.2 merge.1
  15.9 19.7 %all_to_all.36.attended_ref = bf16[32,16,128]{2,1,0:T(8,128)(2,1)S(1)} all-to-all(bf16[32,16,128]{2,1,0:T(8,128)(2,1)S(1)} %merge.1), channel_id=1, replica_groups=mesh['z2'=2,'z1'=2,'z0'=2,'y1'=2,'y0'=2,'ctx'=4,'side'=2] {'z2','z1','z0..., dimensions={0} | all-to-all | bytes 262144 | tf_op jit(solution)/shard_map/all_to_all | solution.py:458
  35.6 0.0 copy-done.5
  35.6 0.0 copy-start
  35.6 0.0 copy-start.4
  35.6 0.2 project.1
  35.9 11.4 %all_to_all.37.came_ref = bf16[8,64,256]{2,1,0:T(8,128)(2,1)S(1)} all-to-all(bf16[8,64,256]{2,1,0:T(8,128)(2,1)S(1)} %project.1), channel_id=1, replica_groups=mesh['z2'=2,'z1'=2,'z0'=2,'y1'=2,'y0'=2,'ctx'=4,'side'=2] {'ctx','side'}, dimensions={0} | all-to-all | bytes 524288 | tf_op jit(solution)/shard_map/all_to_all | solution.py:459
  47.3 0.0 copy-done
  47.3 0.0 copy-done.1
  47.3 0.0 copy-done.3
  47.3 0.0 copy-done.4
  47.3 0.7 widen.1
  48.0 16.3 %all_to_all.38 = bf16[8,32,1920]{2,1,0:T(8,128)(2,1)S(1)} all-to-all(bf16[8,32,1920]{2,1,0:T(8,128)(2,1)S(1)} %get-tuple-element.8), channel_id=1, replica_groups=mesh['z2'=2,'z1'=2,'z0'=2,'y1'=2,'y0'=2,'ctx'=4,'side'=2] {'y1','y0','z0'}, dimensions={0} | all-to-all | bytes 1966080 | tf_op jit(solution)/shard_map/all_to_all | solution.py:463
  64.3 0.1 reduce_sum.21
  64.4 9.7 %all_to_all.39.came_ref = bf16[4,8,1920]{2,1,0:T(8,128)(2,1)S(1)} all-to-all(bf16[4,8,1920]{2,1,0:T(8,128)(2,1)S(1)} %bitcast.9), channel_id=1, replica_groups=mesh['z2'=2,'z1'=2,'z0'=2,'y1'=2,'y0'=2,'ctx'=4,'side'=2] {'z2','z1'}, dimensions={0} | all-to-all | bytes 245760 | tf_op jit(solution)/shard_map/all_to_all | solution.py:465
  74.1 0.2 finish.1
  74.4 14.1 %all_to_all.40.hidden_ref = bf16[32,8,896]{2,1,0:T(8,128)(2,1)S(1)} all-to-all(bf16[32,8,896]{2,1,0:T(8,128)(2,1)S(1)} %finish.1), channel_id=1, replica_groups={{0,248,208,168,128,120,80,40,24,240,200,160,152,112,72,32,16,232,192,18..., dimensions={0} | all-to-all | bytes 917504 | tf_op jit(solution)/shard_map/all_to_all | solution.py:78
  88.5 0.0 copy-done.2
  88.5 0.4 narrow.1
  88.9 12.8 %all_to_all.41 = bf16[8,8,256]{2,1,0:T(8,128)(2,1)S(1)} all-to-all(bf16[8,8,256]{2,1,0:T(8,128)(2,1)S(1)} %bitcast.5), channel_id=1, replica_groups=mesh['z2'=2,'z1'=2,'z0'=2,'y1'=2,'y0'=2,'ctx'=4,'side'=2] {'ctx','side'}, dimensions={0} | all-to-all | bytes 65536 | tf_op jit(solution)/shard_map/all_to_all | solution.py:468
  101.7 0.6 add_convert_fusion
  (4 shorter events, 0.0 us)
Async XLA Ops:
  15.7 19.9 %copy-start.5 = (bf16[1024,256]{1,0:T(8,128)(2,1)S(1)}, bf16[1024,256]{1,0:T(8,128)(2,1)}, u32[]{:S(2)}) copy-start(bf16[1024,256]{1,0:T(8,128)(2,1)} %weight_ref.1) | copy-start | bytes 1572868
  35.6 11.6 %copy-start = (bf16[256,3584]{1,0:T(8,128)(2,1)S(1)}, bf16[256,3584]{1,0:T(8,128)(2,1)}, u32[]{:S(2)}) copy-start(bf16[256,3584]{1,0:T(8,128)(2,1)} %gate_ref.1) | copy-start | bytes 5505028
  35.6 11.6 %copy-start.1 = (bf16[256,3584]{1,0:T(8,128)(2,1)S(1)}, bf16[256,3584]{1,0:T(8,128)(2,1)}, u32[]{:S(2)}) copy-start(bf16[256,3584]{1,0:T(8,128)(2,1)} %up_ref.1) | copy-start | bytes 5505028
  35.6 11.6 %copy-start.3 = (bf16[64,256]{1,0:T(8,128)(2,1)S(1)}, bf16[64,256]{1,0:T(8,128)(2,1)}, u32[]{:S(2)}) copy-start(bf16[64,256]{1,0:T(8,128)(2,1)} %residual_ref.1) | copy-start | bytes 98308
  35.6 11.6 %copy-start.4 = (f32[256]{0:T(256)S(1)}, f32[256]{0:T(256)}, u32[]{:S(2)}) copy-start(f32[256]{0:T(256)} %param.22) | copy-start | bytes 3076
  64.3 24.2 %copy-start.2 = (bf16[3584,256]{1,0:T(8,128)(2,1)S(1)}, bf16[3584,256]{1,0:T(8,128)(2,1)}, u32[]{:S(2)}) copy-start(bf16[3584,256]{1,0:T(8,128)(2,1)} %down_ref.1) | copy-start | bytes 5505028
